TPU v7x, 32 devices: a whole 2x2x4 slice. The times are simulated.
32 devices in a mesh: dp: 8 (over z, x), mp: 4 (over y, core).
Axes of the slice: x: 2, y: 2, z: 4, core: 2. Of those that a mesh axis runs over, the one named last changes fastest.
Arguments:
- rows: bfloat16 [16384, 768], P(('dp', 'mp')), may hold values from -6 to 6
- cotangent: bfloat16 [16384, 768], P(('dp', 'mp')), may hold values from -6 to 6
- group_ids: int32 [64], P(('dp', 'mp')), may hold values from 0 to 7, as said below
- qkv_weight: bfloat16 [3, 768, 768], P(None, None, 'mp'), may hold values from -0.21875 to 0.21875
- out_weight: bfloat16 [768, 768], P('mp'), may hold values from -1.25 to 1.25
- in_weight: bfloat16 [768, 3072], P(None, 'mp'), may hold values from -0.21875 to 0.21875
- down_weight: bfloat16 [3072, 768], P('mp'), may hold values from -0.109375 to 0.109375
- vectors: float32 [6, 768], replicated
- qkv_master: float32 [3, 768, 768], P(None, 'dp', 'mp')
- qkv_first: float32 [3, 768, 768], P(None, 'dp', 'mp'), may hold values from -384 to 384
- qkv_second: float32 [3, 768, 768], P(None, 'dp', 'mp'), may hold values from 4096 to 16384
- out_master: float32 [768, 768], P('mp', 'dp')
- out_first: float32 [768, 768], P('mp', 'dp'), may hold values from -112 to 112
- out_second: float32 [768, 768], P('mp', 'dp'), may hold values from 368.64 to 1474.56
- in_master: float32 [768, 3072], P('dp', 'mp')
- in_first: float32 [768, 3072], P('dp', 'mp'), may hold values from -224 to 224
- in_second: float32 [768, 3072], P('dp', 'mp'), may hold values from 1474.56 to 5898.24
- down_master: float32 [3072, 768], P('mp', 'dp')
- down_first: float32 [3072, 768], P('mp', 'dp'), may hold values from -448 to 448
- down_second: float32 [3072, 768], P('mp', 'dp'), may hold values from 5898.24 to 23592.96
- vec_first: float32 [6, 768], replicated, may hold values from -768 to 768
- vec_second: float32 [6, 768], replicated, may hold values from 16384 to 65536
Outputs:
- out_rows: bfloat16 [16384, 768], P(('dp', 'mp'))
- input_grad: float32 [16384, 768], P(('dp', 'mp'))
- qkv_grad: float32 [3, 768, 768], P(None, 'dp', 'mp')
- out_grad: float32 [768, 768], P('mp', 'dp')
- in_grad: float32 [768, 3072], P('dp', 'mp')
- down_grad: float32 [3072, 768], P('mp', 'dp')
- qkv_first_new: float32 [3, 768, 768], P(None, 'dp', 'mp')
- qkv_second_new: float32 [3, 768, 768], P(None, 'dp', 'mp')
- qkv_new: float32 [3, 768, 768], P(None, 'dp', 'mp')
- out_first_new: float32 [768, 768], P('mp', 'dp')
- out_second_new: float32 [768, 768], P('mp', 'dp')
- out_new: float32 [768, 768], P('mp', 'dp')
- in_first_new: float32 [768, 3072], P('dp', 'mp')
- in_second_new: float32 [768, 3072], P('dp', 'mp')
- in_new: float32 [768, 3072], P('dp', 'mp')
- down_first_new: float32 [3072, 768], P('mp', 'dp')
- down_second_new: float32 [3072, 768], P('mp', 'dp')
- down_new: float32 [3072, 768], P('mp', 'dp')
- vec_grad: float32 [6, 768], replicated
- vec_first_new: float32 [6, 768], replicated
- vec_second_new: float32 [6, 768], replicated
- vec_new: float32 [6, 768], replicated
- matrix_norms: float32 [3, 4], replicated
Inputs may be any that keep to these rules, and one draw needn't show every extreme that they name: group_ids never fall from one image to the next; every group holds at least max(1, 1) images.
All inputs are finite; a program needn't handle non-finite values.
Results may differ from a plain program's by a relative error of at most 0.014.
Values may be sent and summed in bfloat16 or wider, within the bound.
No kernel may reach another device: no remote copies, remote signals or barrier semaphores. Data moves between devices by JAX's collectives and lax.ppermute only.
A program may use at most 128 MiB of HBM per device.

v0:
```python
from functools import partial

import jax
import jax.numpy as jnp
from jax import lax
from jax.sharding import PartitionSpec as P

HEAD_DIM = 64
PATCHES = 256
IMG_BLOCK = 4
GROUPS = 8
STEP = 5


NORM_EPS = 1e-06
ADAM_EPS = 1e-06
MOMENT_DECAY = 0.5
LEARN_RATE = 0.5
WEIGHT_DECAY = 0.01


def layer_stats(values):
    center = values - jnp.mean(values, axis=-1, keepdims=True)
    inverse = lax.rsqrt(jnp.mean(center * center, axis=-1, keepdims=True) + NORM_EPS)
    return (center * inverse, inverse)


def norm_back(grad_normed, normed, inverse):
    return inverse * (
        grad_normed
        - jnp.mean(grad_normed, axis=-1, keepdims=True)
        - normed * jnp.mean(grad_normed * normed, axis=-1, keepdims=True)
    )


def dot_cols(left, right):
    return lax.dot_general(
        left, right, (((0,), (0,)), ((), ())), preferred_element_type=jnp.float32
    )


def dot_back(left, right):
    return lax.dot_general(
        left, right, (((1,), (1,)), ((), ())), preferred_element_type=jnp.float32
    )


def split_blocks(packed):
    images = packed.shape[-2] // PATCHES
    block_size = min(IMG_BLOCK, images)
    heads_here = packed.shape[-1] // HEAD_DIM
    shaped = packed.reshape(
        packed.shape[:-2] + (images // block_size, block_size, PATCHES, heads_here, HEAD_DIM)
    )
    return (shaped, heads_here)


def attend(qkv_low):
    shaped, heads_here = split_blocks(qkv_low)
    shaped = jnp.moveaxis(shaped, 1, 0)
    scale = HEAD_DIM ** (-0.5)

    def one_block(piece):
        scores = (
            jnp.einsum("bqhd,bkhd->bhqk", piece[0], piece[1], preferred_element_type=jnp.float32)
            * scale
        )
        peak = jnp.max(scores, axis=-1, keepdims=True)
        expo = jnp.exp(scores - peak)
        total = jnp.sum(expo, axis=-1, keepdims=True)
        probs_low = (expo / total).astype(jnp.bfloat16)
        mixed = jnp.einsum(
            "bhqk,bkhd->bqhd", probs_low, piece[2], preferred_element_type=jnp.float32
        )
        return (mixed.astype(jnp.bfloat16), peak, total)

    mixed, peaks, totals = lax.map(one_block, shaped)
    return (mixed.reshape(-1, heads_here * HEAD_DIM), peaks, totals)


def attend_back(qkv_low, grad_mixed_low, peaks, totals):
    shaped, heads_here = split_blocks(qkv_low)
    shaped = jnp.moveaxis(shaped, 1, 0)
    grad_shaped, unused_heads = split_blocks(grad_mixed_low)
    scale = HEAD_DIM ** (-0.5)

    def one_block(items):
        piece, grad_block, peak, total = items
        scores = (
            jnp.einsum("bqhd,bkhd->bhqk", piece[0], piece[1], preferred_element_type=jnp.float32)
            * scale
        )
        probs = jnp.exp(scores - peak) / total
        probs_low = probs.astype(jnp.bfloat16)
        grad_probs = jnp.einsum(
            "bqhd,bkhd->bhqk", grad_block, piece[2], preferred_element_type=jnp.float32
        )
        grad_values = jnp.einsum(
            "bhqk,bqhd->bkhd", probs_low, grad_block, preferred_element_type=jnp.float32
        )
        grad_scores = probs * (grad_probs - jnp.sum(probs * grad_probs, axis=-1, keepdims=True))
        grad_low = (grad_scores * scale).astype(jnp.bfloat16)
        grad_queries = jnp.einsum(
            "bhqk,bkhd->bqhd", grad_low, piece[1], preferred_element_type=jnp.float32
        )
        grad_keys = jnp.einsum(
            "bhqk,bqhd->bkhd", grad_low, piece[0], preferred_element_type=jnp.float32
        )
        return jnp.stack([grad_queries, grad_keys, grad_values]).astype(jnp.bfloat16)

    result = lax.map(one_block, (shaped, grad_shaped, peaks, totals))
    result = jnp.moveaxis(result, 1, 0)
    return result.reshape(3, -1, heads_here * HEAD_DIM)


def lamb_parts(grad, master, first, second, correction):
    first_new = MOMENT_DECAY * first + (1.0 - MOMENT_DECAY) * grad
    second_new = MOMENT_DECAY * second + (1.0 - MOMENT_DECAY) * grad * grad
    update = (
        first_new / correction / (jnp.sqrt(second_new / correction) + ADAM_EPS)
        + WEIGHT_DECAY * master
    )
    return (first_new, second_new, update)


def shards(
    rows,
    cotangent,
    group_ids,
    qkv_weight,
    out_weight,
    in_weight,
    down_weight,
    vectors,
    qkv_master,
    qkv_first,
    qkv_second,
    out_master,
    out_first,
    out_second,
    in_master,
    in_first,
    in_second,
    down_master,
    down_first,
    down_second,
    vec_first,
    vec_second,
):
    local_rows = rows.shape[0]
    width = rows.shape[1]
    masters = (qkv_master, out_master, in_master, down_master)
    onehot = (group_ids[:, None] == jnp.arange(GROUPS, dtype=jnp.int32)[None, :]).astype(
        jnp.float32
    )
    weight_squares = jnp.stack([jnp.sum(master * master) for master in masters])
    counts, weight_squares = lax.psum((jnp.sum(onehot, axis=0), weight_squares), ("dp", "mp"))
    qkv_use, out_use, in_use, down_use = (qkv_weight, out_weight, in_weight, down_weight)
    inputs = rows.astype(jnp.float32)
    normed1, inverse1 = layer_stats(inputs)
    normed_in = (normed1 * vectors[0] + vectors[1]).astype(jnp.bfloat16)
    normed_all = lax.all_gather(normed_in, "mp", axis=0, tiled=True)
    qkv_low = jnp.einsum(
        "rd,tdc->trc", normed_all, qkv_use, preferred_element_type=jnp.float32
    ).astype(jnp.bfloat16)
    mixed_low, peaks, totals = attend(qkv_low)
    first = (
        inputs
        + lax.psum_scatter(
            jnp.dot(mixed_low, out_use, preferred_element_type=jnp.float32),
            "mp",
            scatter_dimension=0,
            tiled=True,
        )
        + vectors[4]
    )
    normed2, inverse2 = layer_stats(first)
    normed_mid = (normed2 * vectors[2] + vectors[3]).astype(jnp.bfloat16)
    mid_all = lax.all_gather(normed_mid, "mp", axis=0, tiled=True)
    pre_act = jnp.dot(mid_all, in_use, preferred_element_type=jnp.float32)
    activ, gelu_back = jax.vjp(partial(jax.nn.gelu, approximate=False), pre_act)
    activ_low = activ.astype(jnp.bfloat16)
    result = (
        first
        + lax.psum_scatter(
            jnp.dot(
                lax.dynamic_slice_in_dim(
                    activ_low, jnp.int32(0), local_rows * lax.axis_size("mp"), 0
                ),
                down_use,
                preferred_element_type=jnp.float32,
            ).astype(jnp.bfloat16),
            "mp",
            scatter_dimension=0,
            tiled=True,
        ).astype(jnp.float32)
        + vectors[5]
    )
    out_rows = result.astype(jnp.bfloat16)
    image_weight = jnp.sqrt(
        jnp.sum(counts) / (GROUPS * jnp.dot(onehot, counts, precision=lax.Precision.HIGHEST))
    )
    images_here = group_ids.shape[0]
    grad_out = (
        cotangent.astype(jnp.float32).reshape(images_here, -1, width) * image_weight[:, None, None]
    ).reshape(local_rows, width)
    grad_out_all = lax.all_gather(grad_out.astype(jnp.bfloat16), "mp", axis=0, tiled=True)
    down_part = dot_cols(activ_low, grad_out_all)
    grad_activ = dot_back(grad_out_all, down_use)
    grad_pre = gelu_back(grad_activ)[0]
    grad_pre_low = grad_pre.astype(jnp.bfloat16)
    in_part = dot_cols(mid_all, grad_pre_low)
    grad_mid = lax.psum_scatter(
        dot_back(grad_pre_low, in_use), "mp", scatter_dimension=0, tiled=True
    )
    grad_first = grad_out + norm_back(grad_mid * vectors[2], normed2, inverse2)
    grad_first_all = lax.all_gather(grad_first.astype(jnp.bfloat16), "mp", axis=0, tiled=True)
    out_part = dot_cols(mixed_low, grad_first_all)
    grad_mixed_low = dot_back(grad_first_all, out_use).astype(jnp.bfloat16)
    grad_qkv_low = attend_back(qkv_low, grad_mixed_low, peaks, totals)
    qkv_part = jnp.einsum(
        "rd,trc->tdc", normed_all, grad_qkv_low, preferred_element_type=jnp.float32
    )
    grad_in = lax.psum_scatter(
        jnp.einsum("trc,tdc->rd", grad_qkv_low, qkv_use, preferred_element_type=jnp.float32).astype(
            jnp.bfloat16
        ),
        "mp",
        scatter_dimension=0,
        tiled=True,
    ).astype(jnp.float32)
    input_grad = grad_first + norm_back(grad_in * vectors[0], normed1, inverse1)
    vec_local = jnp.stack(
        [
            jnp.sum(grad_in * normed1, axis=0),
            jnp.sum(grad_in, axis=0),
            jnp.sum(grad_mid * normed2, axis=0),
            jnp.sum(grad_mid, axis=0),
            jnp.sum(grad_first, axis=0),
            jnp.sum(grad_out, axis=0),
        ]
    )
    qkv_grad, out_grad, in_grad, down_grad = (
        lax.psum_scatter(qkv_part, "dp", scatter_dimension=1, tiled=True),
        lax.psum_scatter(out_part, "dp", scatter_dimension=1, tiled=True),
        lax.psum_scatter(in_part, "dp", scatter_dimension=0, tiled=True),
        lax.psum_scatter(down_part, "dp", scatter_dimension=1, tiled=True),
    )
    correction = 1.0 - MOMENT_DECAY**STEP
    qkv_res = lamb_parts(qkv_grad, qkv_master, qkv_first, qkv_second, correction)
    out_res = lamb_parts(out_grad, out_master, out_first, out_second, correction)
    in_res = lamb_parts(in_grad, in_master, in_first, in_second, correction)
    down_res = lamb_parts(down_grad, down_master, down_first, down_second, correction)
    every = (qkv_res, out_res, in_res, down_res)
    update_squares = jnp.stack([jnp.sum(entry[2] * entry[2]) for entry in every])
    vec_grad, update_squares = lax.psum((vec_local, update_squares), ("dp", "mp"))
    weight_norms = jnp.sqrt(weight_squares)
    update_norms = jnp.sqrt(update_squares)
    trusts = weight_norms / (update_norms + ADAM_EPS)
    new_masters = [
        masters[index] - LEARN_RATE * trusts[index] * every[index][2] for index in range(4)
    ]
    matrix_norms = jnp.stack([weight_norms, update_norms, trusts])
    vec_first_new = MOMENT_DECAY * vec_first + (1.0 - MOMENT_DECAY) * vec_grad
    vec_second_new = MOMENT_DECAY * vec_second + (1.0 - MOMENT_DECAY) * vec_grad * vec_grad
    vec_new = vectors - LEARN_RATE * (vec_first_new / correction) / (
        jnp.sqrt(vec_second_new / correction) + ADAM_EPS
    )
    return (
        out_rows,
        input_grad,
        qkv_grad,
        out_grad,
        in_grad,
        down_grad,
        qkv_res[0],
        qkv_res[1],
        new_masters[0],
        out_res[0],
        out_res[1],
        new_masters[1],
        in_res[0],
        in_res[1],
        new_masters[2],
        down_res[0],
        down_res[1],
        new_masters[3],
        vec_grad,
        vec_first_new,
        vec_second_new,
        vec_new,
        matrix_norms,
    )


def solution(mesh):
    in_specs = (
        P(("dp", "mp"), None),
        P(("dp", "mp"), None),
        P(("dp", "mp")),
        P(None, None, "mp"),
        P("mp", None),
        P(None, "mp"),
        P("mp", None),
        P(),
        P(None, "dp", "mp"),
        P(None, "dp", "mp"),
        P(None, "dp", "mp"),
        P("mp", "dp"),
        P("mp", "dp"),
        P("mp", "dp"),
        P("dp", "mp"),
        P("dp", "mp"),
        P("dp", "mp"),
        P("mp", "dp"),
        P("mp", "dp"),
        P("mp", "dp"),
        P(),
        P(),
    )
    out_specs = (
        P(("dp", "mp"), None),
        P(("dp", "mp"), None),
        P(None, "dp", "mp"),
        P("mp", "dp"),
        P("dp", "mp"),
        P("mp", "dp"),
        P(None, "dp", "mp"),
        P(None, "dp", "mp"),
        P(None, "dp", "mp"),
        P("mp", "dp"),
        P("mp", "dp"),
        P("mp", "dp"),
        P("dp", "mp"),
        P("dp", "mp"),
        P("dp", "mp"),
        P("mp", "dp"),
        P("mp", "dp"),
        P("mp", "dp"),
        P(),
        P(),
        P(),
        P(),
        P(),
    )
    return jax.shard_map(shards, mesh=mesh, in_specs=in_specs, out_specs=out_specs, check_vma=False)
```

profile of v0, /device:TPU:0, one launch (start us, length us, event | category | flops | bytes accessed | tf_op | source)
XLA Modules:
  0.0 758.7 jit_solution(12620428635542140853)
XLA Ops:
  14.8 31.3 %all-gather.5.cloned.1.call-done = bf16[2048,768]{1,0:T(8,128)(2,1)} async-done(((bf16[512,768]{1,0:T(8,128)(2,1)}), bf16[2048,768]{1,0:T(8,128)(2,1)}) %all-gather.5.cloned.1.call-update) | async-done | bytes 3145744 | tf_op jit(solution)/shard_map/all_gather | solution.py:162
  46.1 3.9 fusion.98
  50.4 3.0 reshape.179
  55.6 15.6 %while.24 = (s32[]{:T(128)}, bf16[2,4,256,3,64]{2,1,0,4,3:T(4,128)(2,1)}, f32[2,4,3,256,1]{3,2,1,4,0:T(4,128)}, f32[2,4,3,256,1]{3,2,1,4,0:T(4,128)}, bf16[2,3,4...) while((s32[]{:T(128)}, bf16[2,4,256,3,64]{2,1,0,4,3:T(4,128)(2,1)}, ...), condition=%wide.region_5.0_spmd, body=%wide.region_2.5_spmd.sunk | while | flops 208594944 | bytes 24553656 | solution.py:77
  59.7 2.7 fusion.137
  67.5 2.7 fusion.137
  71.2 2.9 reshape.180
  74.1 4.9 fusion.99
  79.1 58.4 %reduce-scatter.13.cloned.1.call-done = f32[512,768]{1,0:T(8,128)} async-done(((f32[2048,768]{1,0:T(8,128)}), f32[512,768]{1,0:T(8,128)}) %reduce-scatter.13.cloned.1.call-update) | async-done | bytes 1572880 | tf_op jit(solution)/shard_map/reduce_scatter | solution.py:169
  142.2 39.7 %psum.28 = f32[8]{0:T(128)S(1)} all-reduce(f32[8]{0:T(128)} %convert_reduce_fusion.2), channel_id=1, replica_groups=mesh['dp'=8,'mp'=4] {'dp','mp'}, use_global_device_ids=true, to_apply=%region_11.0 | all-reduce | flops 8 | bytes 64 | tf_op jit(solution)/shard_map/psum | solution.py:157
  185.5 7.5 fusion.100
  193.0 21.6 %all-gather.9.cloned.1.call-done = bf16[2048,768]{1,0:T(8,128)(2,1)} async-done(((bf16[512,768]{1,0:T(8,128)(2,1)}), bf16[2048,768]{1,0:T(8,128)(2,1)}) %all-gather.9.cloned.1.call-update) | async-done | bytes 3145744 | tf_op jit(solution)/shard_map/all_gather | solution.py:207
  214.5 19.2 %add_convert_fusion = (bf16[2048,768]{1,0:T(8,128)(2,1)S(1)}, f32[2048,768]{1,0:T(8,128)}) fusion(f32[2048,768]{1,0:T(8,128)} %fusion.100, bf16[2048,768]{1,0:T(8,128)(2,1)} %all-gather.9.cloned.1.call-done, bf16[768,768]{1,0:T(8,128)(2,1)S(1)} %copy-done), kind=kOutput, calls=%fused_computation.54 | convolution fusion | flops 2529165312 | bytes 20054016 | tf_op jit(solution)/shard_map/dot_general | solution.py:43
  235.5 4.6 fusion.101
  240.1 5.5 multiply_convert_fusion.1
  247.3 3.9 convolution_convert_fusion
  251.3 47.3 %reduce-scatter.17.cloned.1.call-done = f32[512,768]{1,0:T(8,128)} async-done(((f32[2048,768]{1,0:T(8,128)}), f32[512,768]{1,0:T(8,128)}) %reduce-scatter.17.cloned.1.call-update) | async-done | bytes 1572880 | tf_op jit(solution)/shard_map/reduce_scatter | solution.py:213
  298.6 2.7 multiply_reduce_fusion.2
  301.3 37.7 %reduce-scatter.15.cloned.1.call-done = bf16[512,768]{1,0:T(8,128)(2,1)} async-done(((bf16[2048,768]{1,0:T(8,128)(2,1)}), bf16[512,768]{1,0:T(8,128)(2,1)}) %reduce-scatter.15.cloned.1.call-update) | async-done | bytes 786448 | tf_op jit(solution)/shard_map/reduce_scatter | solution.py:185
  339.0 3.6 fusion.89
  345.1 6.9 fusion.102
  352.1 7.6 fusion.103
  359.8 13.6 %all-gather.11.cloned.1.call-done = bf16[2048,768]{1,0:T(8,128)(2,1)} async-done(((bf16[512,768]{1,0:T(8,128)(2,1)}), bf16[2048,768]{1,0:T(8,128)(2,1)}) %all-gather.11.cloned.1.call-update) | async-done | bytes 3145744 | tf_op jit(solution)/shard_map/all_gather | solution.py:217
  373.4 3.1 convolution_convert_fusion.1
  377.9 4.3 convolution_bitcast_fusion
  382.5 44.7 %while.25 = (s32[]{:T(128)}, bf16[2,3,4,256,3,64]{3,5,4,2,1,0:T(8,128)(2,1)}, bf16[2,3,4,256,3,64]{3,5,4,2,1,0:T(8,128)(2,1)S(1)}, f32[2,4,3,256,1]{3,2,1,4,0:T(...) while((s32[]{:T(128)}, ...), condition=%wide.region_18.19_spmd, body=%wide.region_16.18_spmd.sunk | while | flops 518461952 | bytes 43338416 | solution.py:111
  383.3 2.5 exponential_divide_fusion.2
  389.2 5.5 fusion.144
  394.8 6.4 fusion.143
  401.2 2.5 fusion.141
  411.6 5.5 fusion.144
  417.1 6.4 fusion.143
  423.4 2.6 fusion.141
  427.2 3.5 copy.98
  430.7 3.0 reshape.182
  433.6 4.6 fusion.75
  438.2 2.8 copy.111
  441.0 4.8 reshape.189
  446.1 4.0 bitcast_convert_fusion
  452.3 2.6 multiply_reduce_fusion.10
  455.0 64.5 %reduce-scatter.23.cloned.1.call-done = f32[768,96]{0,1:T(8,128)} async-done(((f32[768,768]{0,1:T(8,128)}), f32[768,96]{0,1:T(8,128)}) %reduce-scatter.23.cloned.1.call-update) | async-done | bytes 294928 | tf_op jit(solution)/shard_map/reduce_scatter | solution.py:247
  519.5 2.8 multiply_reduce_fusion.9
  524.0 60.5 %reduce-scatter.27.cloned.1.call-done = f32[96,192]{1,0:T(8,128)} async-done(((f32[768,192]{1,0:T(8,128)}), f32[96,192]{1,0:T(8,128)}) %reduce-scatter.27.cloned.1.call-update) | async-done | bytes 73744
  586.9 2.7 pad_maximum_fusion.1
  589.6 64.2 %reduce-scatter.25.cloned.1.call-done = f32[96,576]{1,0:T(8,128)} async-done(((f32[768,576]{1,0:T(8,128)}), f32[96,576]{1,0:T(8,128)}) %reduce-scatter.25.cloned.1.call-update) | async-done | bytes 221200
  657.7 2.6 pad_maximum_fusion.2
  660.2 33.1 %reduce-scatter.19.cloned.1.call-done = bf16[512,768]{1,0:T(8,128)(2,1)} async-done(((bf16[2048,768]{1,0:T(8,128)(2,1)}), bf16[512,768]{1,0:T(8,128)(2,1)}) %reduce-scatter.19.cloned.1.call-update) | async-done | bytes 786448 | tf_op jit(solution)/shard_map/reduce_scatter | solution.py:224
  696.3 39.8 %all-reduce = (f32[4]{0:T(128)S(1)}, f32[4]{0:T(128)S(1)}, f32[6,768]{1,0:T(8,128)}) all-reduce(f32[4]{0:T(128)S(1)} %pad_maximum_fusion.2, f32[4]{0:T(128)S(1)} %pad_maximum_fusion.1, f32[6,768]{1,0:T(8,128)S(1)} %stack.91), channel_id=1, replica_groups=mesh['dp'=8,'mp'=4] {'dp','mp'}, use_global_device_ids=true, to_apply=%region_35.36 | all-reduce | flops 4616 | bytes 36928 | tf_op jit(solution)/shard_map/psum | solution.py:256
  (205 shorter events, 75.7 us)
Async XLA Ops:
  7.2 207.4 %copy-start = (bf16[768,768]{1,0:T(8,128)(2,1)S(1)}, bf16[768,768]{1,0:T(8,128)(2,1)}, u32[]{:S(2)}) copy-start(bf16[768,768]{1,0:T(8,128)(2,1)} %param.32) | copy-start | bytes 3538948
  7.2 38.9 %copy-start.46 = (bf16[3,768,192]{1,2,0:T(8,128)(2,1)S(1)}, bf16[3,768,192]{1,2,0:T(8,128)(2,1)}, u32[]{:S(2)}) copy-start(bf16[3,768,192]{1,2,0:T(8,128)(2,1)} %param.29) | copy-start | bytes 2654212
  7.2 38.9 %all-gather.5.cloned.1.call-start = ((), (), s32[]{:S(2)}) async-start(), calls=%async_computation.8 | async-start | bytes 3932160 | tf_op jit(solution)/shard_map/all_gather | solution.py:162
  8.9 2.9 copy-start.29
  14.7 122.9 %reduce-scatter.13.cloned.1.call-start = ((), (), s32[]{:S(2)}) async-start(), calls=%async_computation.9 | async-start | bytes 7864320 | tf_op jit(solution)/shard_map/reduce_scatter | solution.py:169
  71.2 7.8 %copy-start.3 = (bf16[2,3,4,256,3,64]{3,5,4,2,1,0:T(8,128)(2,1)}, bf16[2,3,4,256,3,64]{3,5,4,2,1,0:T(8,128)(2,1)S(1)}, u32[]{:S(2)}) copy-start(bf16[2,3,4,256,3,64]{3,5,4,2,1,0:T(8,128)(2,1)S(1)} %get-tuple-element.435) | copy-start | bytes 7077892
  79.0 58.5 %copy-start.5 = (bf16[512,768]{1,0:T(8,128)(2,1)S(1)}, bf16[512,768]{1,0:T(8,128)(2,1)}, u32[]{:S(2)}) copy-start(bf16[512,768]{1,0:T(8,128)(2,1)} %param.26) | copy-start | bytes 2359300
  79.0 58.5 %copy-start.41 = (f32[768]{0:T(1024)S(1)}, f32[768]{0:T(1024)}, u32[]{:S(2)}) copy-start(f32[768]{0:T(1024)} %get-tuple-element.221) | copy-start | bytes 9220
  79.1 60.5 %copy-start.28 = (f32[768]{0:T(1024)S(1)}, f32[768]{0:T(1024)}, u32[]{:S(2)}) copy-start(f32[768]{0:T(1024)} %get-tuple-element.220) | copy-start | bytes 9220
  79.1 60.5 %copy-start.40 = (f32[768]{0:T(1024)S(1)}, f32[768]{0:T(1024)}, u32[]{:S(2)}) copy-start(f32[768]{0:T(1024)} %get-tuple-element.219) | copy-start | bytes 9220
  79.1 106.4 %all-gather.7.cloned.1.call-start = ((), (), s32[]{:S(2)}) async-start(), calls=%async_computation.10 | async-start | bytes 3932160 | tf_op jit(solution)/shard_map/all_gather | solution.py:179
  139.3 44.8 %copy-start.11 = (bf16[512,768]{1,0:T(8,128)(2,1)S(1)}, bf16[512,768]{1,0:T(8,128)(2,1)}, u32[]{:S(2)}) copy-start(bf16[512,768]{1,0:T(8,128)(2,1)} %param.27) | copy-start | bytes 2359300
  140.8 73.7 %all-gather.9.cloned.1.call-start = ((), (), s32[]{:S(2)}) async-start(), calls=%async_computation.12 | async-start | bytes 3932160 | tf_op jit(solution)/shard_map/all_gather | solution.py:207
  185.2 113.4 %reduce-scatter.17.cloned.1.call-start = ((), (), s32[]{:S(2)}) async-start(), calls=%async_computation.13 | async-start | bytes 7864320 | tf_op jit(solution)/shard_map/reduce_scatter | solution.py:213
  214.5 20.9 %copy-start.45 = (bf16[768,768]{1,0:T(8,128)(2,1)S(1)}, bf16[768,768]{1,0:T(8,128)(2,1)}, u32[]{:S(2)}) copy-start(bf16[768,768]{1,0:T(8,128)(2,1)} %param.31) | copy-start | bytes 3538948
  240.1 98.9 %reduce-scatter.15.cloned.1.call-start = ((), (), s32[]{:S(2)}) async-start(), calls=%async_computation.11 | async-start | bytes 3932160 | tf_op jit(solution)/shard_map/reduce_scatter | solution.py:185
  251.3 87.7 %copy-start.39 = (f32[768]{0:T(1024)S(1)}, f32[768]{0:T(1024)}, u32[]{:S(2)}) copy-start(f32[768]{0:T(1024)} %get-tuple-element.218) | copy-start | bytes 9220
  251.3 122.1 %all-gather.11.cloned.1.call-start = ((), (), s32[]{:S(2)}) async-start(), calls=%async_computation.14 | async-start | bytes 3932160 | tf_op jit(solution)/shard_map/all_gather | solution.py:217
  344.7 107.6 %reduce-scatter.21.cloned.1.call-start = ((), (), s32[]{:S(2)}) async-start(), calls=%async_computation.16 | async-start | bytes 2654208 | tf_op jit(solution)/shard_map/reduce_scatter | solution.py:246
  352.1 21.3 %copy-start.21 = (bf16[192,768]{1,0:T(8,128)(2,1)S(1)}, bf16[192,768]{1,0:T(8,128)(2,1)}, u32[]{:S(2)}) copy-start(bf16[192,768]{1,0:T(8,128)(2,1)} %param.30) | copy-start | bytes 884740
  352.1 167.4 %reduce-scatter.23.cloned.1.call-start = ((), (), s32[]{:S(2)}) async-start(), calls=%async_computation.17 | async-start | bytes 2654208 | tf_op jit(solution)/shard_map/reduce_scatter | solution.py:247
  359.7 224.8 %reduce-scatter.27.cloned.1.call-start = ((), (), s32[]{:S(2)}) async-start(), calls=%async_computation.19 | async-start | bytes 884736
  359.8 18.1 %copy-start.10 = (bf16[2048,192]{0,1:T(8,128)(2,1)S(1)}, bf16[2048,192]{0,1:T(8,128)(2,1)}, u32[]{:S(2)}) copy-start(bf16[2048,192]{0,1:T(8,128)(2,1)} %reshape.180) | copy-start | bytes 2359300
  377.9 4.6 copy-start.4
  382.3 271.6 %reduce-scatter.25.cloned.1.call-start = ((), (), s32[]{:S(2)}) async-start(), calls=%async_computation.18 | async-start | bytes 2211840
  423.4 2.6 copy-start.9
  441.0 5.1 copy-start.14
  441.0 5.1 copy-start.47
  445.8 247.5 %reduce-scatter.19.cloned.1.call-start = ((), (), s32[]{:S(2)}) async-start(), calls=%async_computation.15 | async-start | bytes 3932160 | tf_op jit(solution)/shard_map/reduce_scatter | solution.py:224
  450.2 69.3 %copy-start.17 = (f32[768,96]{0,1:T(8,128)S(1)}, f32[768,96]{0,1:T(8,128)}, u32[]{:S(2)}) copy-start(f32[768,96]{0,1:T(8,128)} %param.43) | copy-start | bytes 884740
  451.1 71.1 %copy-start.38 = (f32[768]{0:T(1024)S(1)}, f32[768]{0:T(1024)}, u32[]{:S(2)}) copy-start(f32[768]{0:T(1024)} %get-tuple-element.252) | copy-start | bytes 9220
  451.1 71.1 %copy-start.37 = (f32[768]{0:T(1024)S(1)}, f32[768]{0:T(1024)}, u32[]{:S(2)}) copy-start(f32[768]{0:T(1024)} %get-tuple-element.274) | copy-start | bytes 9220
  451.1 71.7 %copy-start.36 = (f32[768]{0:T(1024)S(1)}, f32[768]{0:T(1024)}, u32[]{:S(2)}) copy-start(f32[768]{0:T(1024)} %get-tuple-element.204) | copy-start | bytes 9220
  451.1 72.3 %copy-start.35 = (f32[768]{0:T(1024)S(1)}, f32[768]{0:T(1024)}, u32[]{:S(2)}) copy-start(f32[768]{0:T(1024)} %get-tuple-element.209) | copy-start | bytes 9220
  451.1 134.4 %copy-start.19 = (f32[192,96]{1,0:T(8,128)S(1)}, f32[192,96]{1,0:T(8,128)}, u32[]{:S(2)}) copy-start(f32[192,96]{1,0:T(8,128)} %param.37) | copy-start | bytes 221188
  451.1 134.4 %copy-start.26 = (f32[192,96]{1,0:T(8,128)S(1)}, f32[192,96]{1,0:T(8,128)}, u32[]{:S(2)}) copy-start(f32[192,96]{1,0:T(8,128)} %param.38) | copy-start | bytes 221188
  451.1 134.4 %copy-start.27 = (f32[192,96]{1,0:T(8,128)S(1)}, f32[192,96]{1,0:T(8,128)}, u32[]{:S(2)}) copy-start(f32[192,96]{1,0:T(8,128)} %param.39) | copy-start | bytes 221188
  455.0 238.4 %copy-start.6 = (bf16[512,768]{1,0:T(8,128)(2,1)S(1)}, bf16[512,768]{1,0:T(8,128)(2,1)}, u32[]{:S(2)}) copy-start(bf16[512,768]{1,0:T(8,128)(2,1)} %param.26) | copy-start | bytes 2359300
  455.0 238.4 %copy-start.30 = (f32[768]{0:T(1024)S(1)}, f32[768]{0:T(1024)}, u32[]{:S(2)}) copy-start(f32[768]{0:T(1024)} %copy-done.29) | copy-start | bytes 9220
  455.0 238.4 %copy-start.32 = (f32[512]{0:T(512)S(1)}, f32[512]{0:T(512)}, u32[]{:S(2)}) copy-start(f32[512]{0:T(512)} %copy-done.31) | copy-start | bytes 6148
  455.0 238.4 %copy-start.34 = (f32[512]{0:T(512)S(1)}, f32[512]{0:T(512)}, u32[]{:S(2)}) copy-start(f32[512]{0:T(512)} %copy-done.33) | copy-start | bytes 6148
  585.5 4.1 copy-start.20
  586.9 108.4 %copy-start.42 = (f32[1,768]{1,0:T(1,128)S(1)}, f32[1,768]{1,0:T(1,128)}, u32[]{:S(2)}) copy-start(f32[1,768]{1,0:T(1,128)} %stack.90) | copy-start | bytes 9220
  586.9 108.4 %copy-start.43 = (f32[1,768]{1,0:T(1,128)S(1)}, f32[1,768]{1,0:T(1,128)}, u32[]{:S(2)}) copy-start(f32[1,768]{1,0:T(1,128)} %stack.87) | copy-start | bytes 9220
  586.9 108.4 %copy-start.44 = (f32[1,768]{1,0:T(1,128)S(1)}, f32[1,768]{1,0:T(1,128)}, u32[]{:S(2)}) copy-start(f32[1,768]{1,0:T(1,128)} %stack.88) | copy-start | bytes 9220
  660.2 89.7 %copy-start.8 = (f32[512,768]{1,0:T(8,128)S(1)}, f32[512,768]{1,0:T(8,128)}, u32[]{:S(2)}) copy-start(f32[512,768]{1,0:T(8,128)} %copy-done.7) | copy-start | bytes 4718596
  742.0 7.8 %copy-start.12 = (bf16[512,768]{1,0:T(8,128)(2,1)S(1)}, bf16[512,768]{1,0:T(8,128)(2,1)}, u32[]{:S(2)}) copy-start(bf16[512,768]{1,0:T(8,128)(2,1)} %reduce-scatter.19.cloned.1.call-done) | copy-start | bytes 2359300
  744.7 7.0 copy-start.1
  (16 other events, 23.7 us)
Sparse Core Ops, SparseCore 0:
  14.8 31.2 all-gather.4
  79.2 58.3 reduce-scatter.12
  141.0 28.7 all-gather.6
  185.3 29.2 all-gather.8
  240.2 58.3 reduce-scatter.16
  301.0 37.9 reduce-scatter.14
  344.8 28.5 all-gather.10
  377.8 69.0 reduce-scatter.20
  451.4 68.0 reduce-scatter.22
  523.0 61.5 reduce-scatter.26
  588.0 65.8 reduce-scatter.24
  656.4 36.8 reduce-scatter.18
where the time goes:
time: 767 us; the launch traced here: 759 us
  waiting for transfers between devices  432 us (56%)
  matrix products  121 us (16%)
  blocking collectives  79.6 us (10%)
  other arithmetic  53.8 us (7%)
  local copies, waits for them, and re-layouts  52.6 us (7%)
  between operations  17.5 us (2%)
    unnamed x14, waiting for transfers between devices  125 us
    reduce_scatter x1, waiting for transfers between devices, shards(): lax.psum_scatter(down_part, 'dp', scatter_dimension=1, tiled=True)  64.5 us
    reduce_scatter x1, waiting for transfers between devices, shards(): lax.psum_scatter(jnp.dot(mixed_low, out_use, preferred_element_type=jnp.f...  58.4 us
    reduce_scatter x1, waiting for transfers between devices, shards(): lax.psum_scatter(dot_back(grad_pre_low, in_use), 'mp', scatter_dimension=...  47.3 us
    psum x1, blocking collectives, shards(): lax.psum((vec_local, update_squares), ('dp', 'mp'))  39.8 us
    psum x1, blocking collectives, shards(): lax.psum((jnp.sum(onehot, axis=0), weight_squares), ('dp', 'mp'))  39.7 us
    reduce_scatter x1, waiting for transfers between devices, shards(): lax.psum_scatter(jnp.dot(lax.dynamic_slice_in_dim(activ_low, jnp.int32(0)...  37.7 us
    reduce_scatter x1, waiting for transfers between devices, shards(): lax.psum_scatter(jnp.einsum('trc,tdc->rd', grad_qkv_low, qkv_use, preferr...  33.1 us
  transfers between devices with their start and end apart: 12, of which 10 were waited for; matrix products, arithmetic and copies ran while one was open for 18% of the time, Pallas kernels for 0%

commit v1 on v0

v1 whole, which is shorter than its diff:
```python
import math

import jax
import jax.numpy as jnp
from jax import lax
from jax.experimental import pallas as pl
from jax.experimental.pallas import tpu as pltpu
from jax.sharding import PartitionSpec as P

HEAD_DIM = 64
PATCHES = 256
GROUPS = 8
STEP = 5

NORM_EPS = 1e-06
ADAM_EPS = 1e-06
MOMENT_DECAY = 0.5
LEARN_RATE = 0.5
WEIGHT_DECAY = 0.01
SCALE = HEAD_DIM ** (-0.5)

F32 = jnp.float32
BF16 = jnp.bfloat16
MB = 1024 * 1024


def mm(left, right):
    return jnp.dot(left, right, preferred_element_type=F32)


def mm_nt(left, right):
    return lax.dot_general(left, right, (((1,), (1,)), ((), ())), preferred_element_type=F32)


def mm_tn(left, right):
    return lax.dot_general(left, right, (((0,), (0,)), ((), ())), preferred_element_type=F32)


def layer_stats(values):
    center = values - jnp.mean(values, axis=-1, keepdims=True)
    inverse = lax.rsqrt(jnp.mean(center * center, axis=-1, keepdims=True) + NORM_EPS)
    return center * inverse, inverse


def norm_back(grad_normed, normed, inverse):
    return inverse * (
        grad_normed
        - jnp.mean(grad_normed, axis=-1, keepdims=True)
        - normed * jnp.mean(grad_normed * normed, axis=-1, keepdims=True)
    )


def gelu_pair(t):
    size = jnp.abs(t) * (2.0**-0.5)
    k = 1.0 / (1.0 + 0.3275911 * size)
    bell = jnp.exp(-size * size)
    poly = k * (
        0.254829592
        + k * (-0.284496736 + k * (1.421413741 + k * (-1.453152027 + k * 1.061405429)))
    )
    tail = 0.5 * poly * bell
    cdf = jnp.where(t < 0, tail, 1.0 - tail)
    return t * cdf, cdf + t * bell * (1.0 / math.sqrt(2.0 * math.pi))


def put_turned(out_ref, value, pos_ref, count, start):
    turned = value.T
    part = turned.shape[0] // count
    width = turned.shape[1]
    if len(out_ref.shape) == 2:
        out_ref[:, start : start + width] = turned
        return
    for j in range(count):
        out_ref[pos_ref[j], :, start : start + width] = turned[j * part : (j + 1) * part]


def turned_shape(width, rows, count):
    part = width // count
    if part % 16 == 0:
        return (count, part, rows)
    return (width, rows)


def turned_order(turned, pos, count):
    width = turned.shape[0] if turned.ndim == 2 else turned.shape[0] * turned.shape[1]
    rows = turned.shape[-1]
    if turned.ndim == 2:
        shaped = turned.reshape(count, width // count, rows)
        turned = jnp.zeros_like(shaped).at[pos].set(shaped)
    return turned.reshape(width, rows)


def params(limit, **more):
    return pltpu.CompilerParams(vmem_limit_bytes=limit * MB, **more)


def full(shape):
    return pl.BlockSpec(shape, lambda *_: (0,) * len(shape))


SMEM = pl.BlockSpec(memory_space=pltpu.SMEM)


def start_kernel(pos_ref, rows_ref, vec_ref, x_ref, xt_ref, *, count):
    width, rows = rows_ref.shape[1], rows_ref.shape[0]
    for start in range(0, rows, PATCHES):
        normed, _ = layer_stats(rows_ref[start : start + PATCHES].astype(F32))
        low = (normed * vec_ref[0:1] + vec_ref[1:2]).astype(BF16)
        x_ref[start : start + PATCHES] = low
        put_turned(xt_ref, low, pos_ref, count, start)


def run_start(pos, rows, vectors, count):
    r, d = rows.shape
    return pl.pallas_call(
        lambda *refs: start_kernel(*refs, count=count),
        out_shape=(
            jax.ShapeDtypeStruct((r, d), BF16),
            jax.ShapeDtypeStruct(turned_shape(d, r, count), BF16),
        ),
        in_specs=[SMEM, pl.BlockSpec(memory_space=pltpu.VMEM), pl.BlockSpec(memory_space=pltpu.VMEM)],
        compiler_params=params(32),
    )(pos, rows, vectors)


def gout_kernel(pos_ref, weight_ref, cot_ref, g_ref, gt_ref, *, count):
    rows = cot_ref.shape[0]
    for index in range(rows // PATCHES):
        start = index * PATCHES
        low = (cot_ref[start : start + PATCHES].astype(F32) * weight_ref[index]).astype(BF16)
        g_ref[start : start + PATCHES] = low
        put_turned(gt_ref, low, pos_ref, count, start)


def run_gout(pos, weight, cot, count):
    r, d = cot.shape
    return pl.pallas_call(
        lambda *refs: gout_kernel(*refs, count=count),
        out_shape=(
            jax.ShapeDtypeStruct((r, d), BF16),
            jax.ShapeDtypeStruct(turned_shape(d, r, count), BF16),
        ),
        in_specs=[SMEM, SMEM, pl.BlockSpec(memory_space=pltpu.VMEM)],
        compiler_params=params(32),
    )(pos, weight, cot)


def attend_shard(x, w_ref, saved_ref, probs_ref):
    cols = w_ref.shape[1] // 4
    qkv = mm(x, w_ref[:, : 3 * cols]).astype(BF16)
    saved_ref[:, : 3 * cols] = qkv
    mixed = []
    for h in range(cols // HEAD_DIM):
        at = h * HEAD_DIM
        q = qkv[:, at : at + HEAD_DIM] * SCALE
        k = qkv[:, cols + at : cols + at + HEAD_DIM]
        v = qkv[:, 2 * cols + at : 2 * cols + at + HEAD_DIM]
        scores = mm_nt(q, k)
        expo = jnp.exp(scores - jnp.max(scores, axis=-1, keepdims=True))
        probs = (expo * (1.0 / jnp.sum(expo, axis=-1, keepdims=True))).astype(BF16)
        probs_ref[h] = probs
        mixed.append(mm(probs, v).astype(BF16))
    mixed = jnp.concatenate(mixed, axis=1)
    saved_ref[:, 3 * cols :] = mixed
    return mm_nt(mixed, w_ref[:, 3 * cols :])


def attn_one_kernel(x_ref, rows_ref, vec_ref, wa_ref, wb_ref, acc_ref, sa_ref, pa_ref, sb_ref, pb_ref):
    x = x_ref[...]
    term = attend_shard(x, wa_ref, sa_ref, pa_ref)
    term += attend_shard(x, wb_ref, sb_ref, pb_ref)
    acc_ref[...] = rows_ref[...].astype(F32) + term + vec_ref[4:5]


def attn_two_kernel(
    pos_ref, x_ref, acc_ref, vec_ref, wa_ref, wb_ref,
    first_ref, mid_ref, midt_ref, sa_ref, pa_ref, sb_ref, pb_ref, *, count,
):
    x = x_ref[...]
    term = attend_shard(x, wa_ref, sa_ref, pa_ref)
    term += attend_shard(x, wb_ref, sb_ref, pb_ref)
    first = acc_ref[...] + term
    first_ref[...] = first
    normed, _ = layer_stats(first)
    low = (normed * vec_ref[2:3] + vec_ref[3:4]).astype(BF16)
    mid_ref[...] = low
    put_turned(midt_ref, low, pos_ref, count, 0)


def image_block(d):
    return pl.BlockSpec((PATCHES, d), lambda i: (i, 0))


def saved_outputs(r, d, heads):
    images = r // PATCHES
    shapes = (
        jax.ShapeDtypeStruct((r, d), BF16),
        jax.ShapeDtypeStruct((images * heads, PATCHES, PATCHES), BF16),
    )
    specs = [image_block(d), pl.BlockSpec((heads, PATCHES, PATCHES), lambda i: (i, 0, 0))]
    return shapes, specs


def attn_cost(r, d):
    return pl.CostEstimate(flops=2 * 2 * r * d * d + 8 * r * PATCHES * d // 2, bytes_accessed=10 * MB, transcendentals=r * PATCHES * 6)


def run_attn_one(x, rows, vectors, wa, wb):
    r, d = x.shape
    heads = d // 4 // HEAD_DIM
    shapes, specs = saved_outputs(r, d, heads)
    return pl.pallas_call(
        attn_one_kernel,
        grid=(r // PATCHES,),
        out_shape=(jax.ShapeDtypeStruct((r, d), F32),) + shapes * 2,
        in_specs=[image_block(d), image_block(d), full(vectors.shape), full((d, d)), full((d, d))],
        out_specs=[image_block(d)] + specs * 2,
        compiler_params=params(32),
        cost_estimate=attn_cost(r, d),
    )(x, rows, vectors, wa, wb)


def run_attn_two(pos, x, acc, vectors, wa, wb, count):
    r, d = x.shape
    heads = d // 4 // HEAD_DIM
    shapes, specs = saved_outputs(r, d, heads)
    tshape = turned_shape(d, r, count)
    tspec = pl.BlockSpec(
        tshape[:-1] + (PATCHES,), lambda i: (0,) * (len(tshape) - 1) + (i,)
    )
    return pl.pallas_call(
        lambda *refs: attn_two_kernel(*refs, count=count),
        grid=(r // PATCHES,),
        out_shape=(
            jax.ShapeDtypeStruct((r, d), F32),
            jax.ShapeDtypeStruct((r, d), BF16),
            jax.ShapeDtypeStruct(tshape, BF16),
        )
        + shapes * 2,
        in_specs=[SMEM, image_block(d), image_block(d), full(vectors.shape), full((d, d)), full((d, d))],
        out_specs=[image_block(d), image_block(d), tspec] + specs * 2,
        compiler_params=params(32),
        cost_estimate=attn_cost(r, d),
    )(pos, x, acc, vectors, wa, wb)


TILES = 3


def ffn_tile(mid_ref, midt_ref, g_ref, gt_ref, in_ref, down_ref, gi_ref, gd_ref, y_ref, dm_ref):
    w_in = in_ref[...]
    w_down = down_ref[...]
    pre = mm(mid_ref[...], w_in)
    dact = mm_nt(g_ref[...], w_down)
    activ, slope = gelu_pair(pre)
    activ = activ.astype(BF16)
    dpre = (dact * slope).astype(BF16)
    y_ref[...] += mm(activ, w_down)
    dm_ref[...] += mm_nt(dpre, w_in)
    gd_ref[...] = mm(gt_ref[...], activ).astype(BF16)
    gi_ref[...] = mm(midt_ref[...], dpre).astype(BF16)


def ffn_pair(mid_ref, midt_ref, g_ref, gt_ref, wa, wb, ga, gb, y_ref, dm_ref):
    step = pl.program_id(0)

    @pl.when(step < TILES)
    def _():
        ffn_tile(mid_ref, midt_ref, g_ref, gt_ref, *wa, *ga, y_ref, dm_ref)

    @pl.when(step >= TILES)
    def _():
        ffn_tile(mid_ref, midt_ref, g_ref, gt_ref, *wb, *gb, y_ref, dm_ref)


def ffn_one_kernel(
    mid_ref, midt_ref, g_ref, gt_ref, ia_ref, da_ref, ib_ref, db_ref,
    y_ref, dm_ref, gia_ref, gda_ref, gib_ref, gdb_ref,
):
    @pl.when(pl.program_id(0) == 0)
    def _():
        y_ref[...] = jnp.zeros_like(y_ref)
        dm_ref[...] = jnp.zeros_like(dm_ref)

    ffn_pair(
        mid_ref, midt_ref, g_ref, gt_ref, (ia_ref, da_ref), (ib_ref, db_ref),
        (gia_ref, gda_ref), (gib_ref, gdb_ref), y_ref, dm_ref,
    )


def ffn_two_kernel(
    pos_ref, weight_ref, mid_ref, midt_ref, g_ref, gt_ref, ia_ref, da_ref, ib_ref, db_ref,
    y_in_ref, dm_in_ref, first_ref, cot_ref, vec_ref,
    out_ref, gf_ref, gfl_ref, gft_ref, sums_ref, gia_ref, gda_ref, gib_ref, gdb_ref,
    y_ref, dm_ref, *, count,
):
    @pl.when(pl.program_id(0) == 0)
    def _():
        y_ref[...] = y_in_ref[...]
        dm_ref[...] = dm_in_ref[...]

    ffn_pair(
        mid_ref, midt_ref, g_ref, gt_ref, (ia_ref, da_ref), (ib_ref, db_ref),
        (gia_ref, gda_ref), (gib_ref, gdb_ref), y_ref, dm_ref,
    )

    @pl.when(pl.program_id(0) == pl.num_programs(0) - 1)
    def _():
        rows = first_ref.shape[0]
        sums = [0.0, 0.0, 0.0, 0.0]
        chunk = 128
        for start in range(0, rows, chunk):
            here = slice(start, start + chunk)
            first = first_ref[here]
            normed, inverse = layer_stats(first)
            out_ref[here] = (first + y_ref[here] + vec_ref[5:6]).astype(BF16)
            dmid = dm_ref[here]
            gout = cot_ref[here].astype(F32) * weight_ref[start // PATCHES]
            gfirst = gout + norm_back(dmid * vec_ref[2:3], normed, inverse)
            gf_ref[here] = gfirst
            low = gfirst.astype(BF16)
            gfl_ref[here] = low
            put_turned(gft_ref, low, pos_ref, count, start)
            for index, term in enumerate((dmid * normed, dmid, gfirst, gout)):
                sums[index] += jnp.sum(term, axis=0, keepdims=True)
        sums_ref[...] = jnp.concatenate(sums + sums, axis=0)


def ffn_specs(d):
    tile = d // TILES
    cols = lambda f: pl.BlockSpec((d, tile), lambda i: (0, f(i)))
    rows = lambda f: pl.BlockSpec((tile, d), lambda i: (f(i), 0))
    fa = lambda i: jnp.minimum(i, TILES - 1)
    fb = lambda i: jnp.maximum(i - TILES, 0)
    return [cols(fa), rows(fa), cols(fb), rows(fb)], [cols(fa), cols(fa), cols(fb), cols(fb)]


def ffn_cost(r, d):
    return pl.CostEstimate(flops=2 * 7 * 2 * r * d * d, bytes_accessed=16 * MB, transcendentals=4 * r * d)


def run_ffn_one(mid, midt, g, gt, wa, wb):
    r, d = mid.shape
    w_specs, g_specs = ffn_specs(d)
    grad = jax.ShapeDtypeStruct((d, d), BF16)
    return pl.pallas_call(
        ffn_one_kernel,
        grid=(2 * TILES,),
        out_shape=(jax.ShapeDtypeStruct((r, d), F32),) * 2 + (grad,) * 4,
        in_specs=[full((r, d)), full((d, r)), full((r, d)), full((d, r))] + w_specs,
        out_specs=[full((r, d)), full((r, d))] + g_specs,
        compiler_params=params(40),
        cost_estimate=ffn_cost(r, d),
    )(mid, midt, g, gt, *wa, *wb)


def run_ffn_two(pos, weight, mid, midt, g, gt, wa, wb, y, dm, first, cot, vectors, count):
    r, d = mid.shape
    w_specs, g_specs = ffn_specs(d)
    grad = jax.ShapeDtypeStruct((d, d), BF16)
    tshape = turned_shape(d, r, count)
    return pl.pallas_call(
        lambda *refs: ffn_two_kernel(*refs, count=count),
        grid=(2 * TILES,),
        out_shape=(
            jax.ShapeDtypeStruct((r, d), BF16),
            jax.ShapeDtypeStruct((r, d), F32),
            jax.ShapeDtypeStruct((r, d), BF16),
            jax.ShapeDtypeStruct(tshape, BF16),
            jax.ShapeDtypeStruct((8, d), F32),
        )
        + (grad,) * 4,
        in_specs=[SMEM, SMEM, full((r, d)), full((d, r)), full((r, d)), full((d, r))]
        + w_specs
        + [full((r, d))] * 4
        + [full(vectors.shape)],
        out_specs=[full((r, d)), full((r, d)), full((r, d)), full(tshape), full((8, d))] + g_specs,
        scratch_shapes=[pltpu.VMEM((r, d), F32), pltpu.VMEM((r, d), F32)],
        compiler_params=params(52),
        cost_estimate=ffn_cost(r, d),
    )(pos, weight, mid, midt, g, gt, *wa, *wb, y, dm, first, cot, vectors)


def attend_back_shard(gf, w_ref, saved_ref, probs_ref, keep_ref):
    cols = w_ref.shape[1] // 4
    start = pl.multiple_of(pl.program_id(0) * PATCHES, PATCHES)
    dmix = mm(gf, w_ref[:, 3 * cols :]).astype(BF16)
    dq, dk, dv = [], [], []
    for h in range(cols // HEAD_DIM):
        at = h * HEAD_DIM
        q = saved_ref[:, at : at + HEAD_DIM]
        k = saved_ref[:, cols + at : cols + at + HEAD_DIM]
        v = saved_ref[:, 2 * cols + at : 2 * cols + at + HEAD_DIM]
        do = dmix[:, at : at + HEAD_DIM]
        probs = probs_ref[h]
        dv.append(mm_tn(probs, do).astype(BF16))
        dp = mm_nt(do, v)
        wide = probs.astype(F32)
        ds = (SCALE * wide * (dp - jnp.sum(wide * dp, axis=-1, keepdims=True))).astype(BF16)
        dq.append(mm(ds, k).astype(BF16))
        dk.append(mm_tn(ds, q).astype(BF16))
    dqkv = jnp.concatenate(dq + dk + dv, axis=1)
    keep_ref[pl.ds(start, PATCHES), : 3 * cols] = dqkv
    keep_ref[pl.ds(start, PATCHES), 3 * cols :] = saved_ref[:, 3 * cols :]
    return mm_nt(dqkv, w_ref[:, : 3 * cols])


def attn_grad(xt_ref, gft_ref, keep_ref, g_ref):
    cols = keep_ref.shape[1] // 4
    g_ref[:, : 3 * cols] = mm(xt_ref[...], keep_ref[:, : 3 * cols]).astype(BF16)
    g_ref[:, 3 * cols :] = mm(gft_ref[...], keep_ref[:, 3 * cols :]).astype(BF16)


def back_one_kernel(
    gf_ref, xt_ref, gft_ref, wa_ref, wb_ref, sa_ref, pa_ref, sb_ref, pb_ref,
    acc_ref, ga_ref, gb_ref, ka_ref, kb_ref,
):
    gf = gf_ref[...]
    term = attend_back_shard(gf, wa_ref, sa_ref, pa_ref, ka_ref)
    term += attend_back_shard(gf, wb_ref, sb_ref, pb_ref, kb_ref)
    acc_ref[...] = term

    @pl.when(pl.program_id(0) == pl.num_programs(0) - 1)
    def _():
        attn_grad(xt_ref, gft_ref, ka_ref, ga_ref)
        attn_grad(xt_ref, gft_ref, kb_ref, gb_ref)


def back_two_kernel(
    gf_ref, xt_ref, gft_ref, wa_ref, wb_ref, sa_ref, pa_ref, sb_ref, pb_ref,
    acc_ref, rows_ref, gfirst_ref, vec_ref,
    ig_ref, sums_ref, ga_ref, gb_ref, ka_ref, kb_ref,
):
    gf = gf_ref[...]
    term = attend_back_shard(gf, wa_ref, sa_ref, pa_ref, ka_ref)
    term += attend_back_shard(gf, wb_ref, sb_ref, pb_ref, kb_ref)
    grad_in = acc_ref[...] + term
    normed, inverse = layer_stats(rows_ref[...].astype(F32))
    ig_ref[...] = gfirst_ref[...] + norm_back(grad_in * vec_ref[0:1], normed, inverse)
    one = jnp.sum(grad_in * normed, axis=0, keepdims=True)
    two = jnp.sum(grad_in, axis=0, keepdims=True)
    sums = jnp.concatenate([one, two] * 4, axis=0)

    @pl.when(pl.program_id(0) == 0)
    def _():
        sums_ref[...] = sums

    @pl.when(pl.program_id(0) > 0)
    def _():
        sums_ref[...] += sums

    @pl.when(pl.program_id(0) == pl.num_programs(0) - 1)
    def _():
        attn_grad(xt_ref, gft_ref, ka_ref, ga_ref)
        attn_grad(xt_ref, gft_ref, kb_ref, gb_ref)


def back_cost(r, d):
    return pl.CostEstimate(flops=2 * 2 * 2 * r * d * d + 20 * r * PATCHES * d // 2, bytes_accessed=12 * MB, transcendentals=0)


def run_back(gfl, xt, gft, wa, wb, saved_a, saved_b, tail=None):
    r, d = gfl.shape
    heads = d // 4 // HEAD_DIM
    _, specs = saved_outputs(r, d, heads)
    grad = jax.ShapeDtypeStruct((d, d), BF16)
    wide = jax.ShapeDtypeStruct((r, d), F32)
    in_specs = [image_block(d), full((d, r)), full((d, r)), full((d, d)), full((d, d))] + specs * 2
    scratch = [pltpu.VMEM((r, d), BF16)] * 2
    if tail is None:
        return pl.pallas_call(
            back_one_kernel,
            grid=(r // PATCHES,),
            out_shape=(wide, grad, grad),
            in_specs=in_specs,
            out_specs=[image_block(d), full((d, d)), full((d, d))],
            scratch_shapes=scratch,
            compiler_params=params(40),
            cost_estimate=back_cost(r, d),
        )(gfl, xt, gft, wa, wb, *saved_a, *saved_b)
    return pl.pallas_call(
        back_two_kernel,
        grid=(r // PATCHES,),
        out_shape=(wide, jax.ShapeDtypeStruct((8, d), F32), grad, grad),
        in_specs=in_specs + [image_block(d)] * 3 + [full(tail[3].shape)],
        out_specs=[image_block(d), full((8, d)), full((d, d)), full((d, d))],
        scratch_shapes=scratch,
        compiler_params=params(40),
        cost_estimate=back_cost(r, d),
    )(gfl, xt, gft, wa, wb, *saved_a, *saved_b, *tail)


def swap(value, axis, bit):
    size = lax.axis_size(axis)
    return lax.ppermute(value, axis, [(i, i ^ bit) for i in range(size)])


def all_sum(value):
    for axis in ("mp", "dp"):
        bit = 1
        while bit < lax.axis_size(axis):
            value = value + swap(value, axis, bit)
            bit *= 2
    return value


def reduce_parts(g0, g1, g2, g3, bits):
    c1 = swap(g1, "mp", 1)
    c3 = swap(g3, "mp", 1)
    s2 = (g2.astype(F32) + c3.astype(F32)).astype(BF16)
    y2 = swap(s2, "mp", 2)
    total = g0.astype(F32) + c1.astype(F32) + y2.astype(F32)
    for bit in bits:
        half = total.shape[0] // 2
        total = total[:half] + swap(total[half:].astype(BF16), "dp", 1 << bit).astype(F32)
    return total


def lamb_parts(grad, master, first, second, correction):
    first_new = MOMENT_DECAY * first + (1.0 - MOMENT_DECAY) * grad
    second_new = MOMENT_DECAY * second + (1.0 - MOMENT_DECAY) * grad * grad
    update = (
        first_new / correction / (jnp.sqrt(second_new / correction) + ADAM_EPS)
        + WEIGHT_DECAY * master
    )
    return (first_new, second_new, update)


def shards(
    rows,
    cotangent,
    group_ids,
    qkv_weight,
    out_weight,
    in_weight,
    down_weight,
    vectors,
    qkv_master,
    qkv_first,
    qkv_second,
    out_master,
    out_first,
    out_second,
    in_master,
    in_first,
    in_second,
    down_master,
    down_first,
    down_second,
    vec_first,
    vec_second,
):
    count = lax.axis_size("dp")
    width = rows.shape[1]
    cols = qkv_weight.shape[2]
    nbits = count.bit_length() - 1
    bits = tuple(range(nbits))
    rel = jnp.arange(count, dtype=jnp.int32) ^ lax.axis_index("dp").astype(jnp.int32)
    pos = sum(((rel >> bit) & 1) << (nbits - 1 - place) for place, bit in enumerate(bits))

    attn_w = [
        jnp.concatenate([qkv_weight[0], qkv_weight[1], qkv_weight[2], out_weight.T], axis=1)
    ]
    in_w = [in_weight]
    down_w = [down_weight]
    for group in (attn_w, in_w, down_w):
        near = swap(group[0], "mp", 1)
        far = swap(group[0], "mp", 2)
        group += [near, far, swap(far, "mp", 1)]

    onehot = (group_ids[:, None] == jnp.arange(GROUPS, dtype=jnp.int32)[None, :]).astype(F32)
    counts = all_sum(jnp.sum(onehot, axis=0))
    image_weight = jnp.sqrt(jnp.sum(counts) / (GROUPS * jnp.sum(onehot * counts, axis=1)))

    x, xt = run_start(pos, rows, vectors, count)
    xt = turned_order(xt, pos, count)
    gout, goutt = run_gout(pos, image_weight, cotangent, count)
    goutt = turned_order(goutt, pos, count)
    acc, s1, p1, s0, p0 = run_attn_one(x, rows, vectors, attn_w[1], attn_w[0])
    first, mid, midt, s3, p3, s2, p2 = run_attn_two(pos, x, acc, vectors, attn_w[3], attn_w[2], count)
    midt = turned_order(midt, pos, count)
    y, dm, gi1, gd1, gi0, gd0 = run_ffn_one(
        mid, midt, gout, goutt, (in_w[1], down_w[1]), (in_w[0], down_w[0])
    )
    out_rows, gfirst, gfl, gft, sums_b, gi3, gd3, gi2, gd2 = run_ffn_two(
        pos, image_weight, mid, midt, gout, goutt, (in_w[3], down_w[3]), (in_w[2], down_w[2]),
        y, dm, first, cotangent, vectors, count,
    )
    gft = turned_order(gft, pos, count)
    gin, ga3, ga2 = run_back(gfl, xt, gft, attn_w[3], attn_w[2], (s3, p3), (s2, p2))
    input_grad, sums_a, ga1, ga0 = run_back(
        gfl, xt, gft, attn_w[1], attn_w[0], (s1, p1), (s0, p0), (gin, rows, gfirst, vectors)
    )
    down_sum = reduce_parts(gd0, gd1, gd2, gd3, bits)
    in_sum = reduce_parts(gi0, gi1, gi2, gi3, bits)
    attn_sum = reduce_parts(ga0, ga1, ga2, ga3, bits)

    part = width // count
    qkv_grad = jnp.moveaxis(attn_sum[:, : 3 * cols].reshape(part, 3, cols), 1, 0)
    out_grad = attn_sum[:, 3 * cols :].T
    in_grad = in_sum
    down_grad = down_sum.T

    correction = 1.0 - MOMENT_DECAY**STEP
    qkv_res = lamb_parts(qkv_grad, qkv_master, qkv_first, qkv_second, correction)
    out_res = lamb_parts(out_grad, out_master, out_first, out_second, correction)
    in_res = lamb_parts(in_grad, in_master, in_first, in_second, correction)
    down_res = lamb_parts(down_grad, down_master, down_first, down_second, correction)
    every = (qkv_res, out_res, in_res, down_res)
    masters = (qkv_master, out_master, in_master, down_master)
    squares = jnp.stack(
        [jnp.sum(master * master) for master in masters]
        + [jnp.sum(entry[2] * entry[2]) for entry in every]
    )
    squares = jnp.pad(squares[None], ((0, 1), (0, width - 8)))
    small = all_sum(jnp.concatenate([sums_a[:2], sums_b[:4], squares], axis=0))
    vec_grad = small[:6]
    weight_norms = jnp.sqrt(small[6, :4])
    update_norms = jnp.sqrt(small[6, 4:8])
    trusts = weight_norms / (update_norms + ADAM_EPS)
    new_masters = [
        masters[index] - LEARN_RATE * trusts[index] * every[index][2] for index in range(4)
    ]
    matrix_norms = jnp.stack([weight_norms, update_norms, trusts])
    vec_first_new = MOMENT_DECAY * vec_first + (1.0 - MOMENT_DECAY) * vec_grad
    vec_second_new = MOMENT_DECAY * vec_second + (1.0 - MOMENT_DECAY) * vec_grad * vec_grad
    vec_new = vectors - LEARN_RATE * (vec_first_new / correction) / (
        jnp.sqrt(vec_second_new / correction) + ADAM_EPS
    )
    return (
        out_rows,
        input_grad,
        qkv_grad,
        out_grad,
        in_grad,
        down_grad,
        qkv_res[0],
        qkv_res[1],
        new_masters[0],
        out_res[0],
        out_res[1],
        new_masters[1],
        in_res[0],
        in_res[1],
        new_masters[2],
        down_res[0],
        down_res[1],
        new_masters[3],
        vec_grad,
        vec_first_new,
        vec_second_new,
        vec_new,
        matrix_norms,
    )


def solution(mesh):
    rows = P(("dp", "mp"), None)
    qkv_state = P(None, "dp", "mp")
    out_state = P("mp", "dp")
    in_state = P("dp", "mp")
    in_specs = (
        (rows, rows, P(("dp", "mp")), P(None, None, "mp"), P("mp", None), P(None, "mp"), P("mp", None), P())
        + (qkv_state,) * 3
        + (out_state,) * 3
        + (in_state,) * 3
        + (out_state,) * 3
        + (P(), P())
    )
    out_specs = (
        (rows, rows, qkv_state, out_state, in_state, out_state)
        + (qkv_state,) * 3
        + (out_state,) * 3
        + (in_state,) * 3
        + (out_state,) * 3
        + (P(),) * 5
    )
    return jax.shard_map(shards, mesh=mesh, in_specs=in_specs, out_specs=out_specs, check_vma=False)
```

time: 767 us -> 342 us (0.45)
  waiting for transfers between devices: 432 us -> 154 us
  matrix products: 121 us -> 0 us
  blocking collectives: 79.6 us -> 0 us
  Pallas kernels: 0 us -> 71.2 us
  starting transfers between devices: 1.5 us -> 36.6 us
  other arithmetic: 53.8 us -> 27 us
  between operations: 17.5 us -> 4.04 us
    reduce_scatter x6 -> x0, waiting for transfers between devices: 241 us -> none  [the longest x1 64.5 us: shards(): lax.psum_scatter(down_part, 'dp', scatter_dimension=1, tiled=True)]
    ppermute x0 -> x37, waiting for transfers between devices: none -> 154 us  [swap(): return lax.ppermute(value, axis, [(i, i ^ bit) for i in range(size)])]
    unnamed x14 -> x0, waiting for transfers between devices: 125 us -> none
    dot_general x25 -> x0, matrix products: 113 us -> none  [the longest x3 26.8 us: dot_back(): lax.dot_general(left, right, (((1,), (1,)), ((), ())), preferred_element_...]
    psum x2 -> x0, blocking collectives: 79.6 us -> none  [the longest x1 39.8 us: shards(): lax.psum((vec_local, update_squares), ('dp', 'mp'))]
    pallas_call x0 -> x8, Pallas kernels: none -> 71.2 us  [the longest x1 19.6 us: run_ffn_two(): pl.pallas_call(lambda *refs: ffn_two_kernel(*refs, count=count), grid=(2...]
    all_gather x4 -> x0, waiting for transfers between devices: 66.5 us -> none  [the longest x1 31.3 us: shards(): normed_all = lax.all_gather(normed_in, 'mp', axis=0, tiled=True)]
    ppermute x0 -> x37, starting transfers between devices: none -> 36.6 us  [swap(): return lax.ppermute(value, axis, [(i, i ^ bit) for i in range(size)])]
  transfers between devices with their start and end apart: 12 -> 37, of which waited for: 10 -> 15; matrix products, arithmetic and copies ran while one was open for 18% -> 10% of each run, Pallas kernels for 0% -> 15%
where the time goes in v1:
time: 342 us; the launch traced here: 341 us
  waiting for transfers between devices  154 us (45%)
  Pallas kernels  71.2 us (21%)
  local copies, waits for them, and re-layouts  48 us (14%)
  starting transfers between devices  36.6 us (11%)
  other arithmetic  27 us (8%)
  between operations  4.04 us (1%)
    ppermute x37, waiting for transfers between devices, swap(): return lax.ppermute(value, axis, [(i, i ^ bit) for i in range(size)])  154 us
    unnamed x178, local copies, waits for them, and re-layouts  37.7 us
    ppermute x37, starting transfers between devices, swap(): return lax.ppermute(value, axis, [(i, i ^ bit) for i in range(size)])  36.6 us
    pallas_call x1, Pallas kernels, run_ffn_two(): pl.pallas_call(lambda *refs: ffn_two_kernel(*refs, count=count), grid=(2...  19.6 us
    pallas_call x1, Pallas kernels, run_ffn_one(): pl.pallas_call(ffn_one_kernel, grid=(2 * TILES,), out_shape=(jax.ShapeDty...  14.5 us
    pallas_call x1, Pallas kernels, run_back(): pl.pallas_call(back_one_kernel, grid=(r // PATCHES,), out_shape=(wide, gr...  11.8 us
    pallas_call x1, Pallas kernels, run_back(): pl.pallas_call(back_two_kernel, grid=(r // PATCHES,), out_shape=(wide, ja...  11.7 us
    pallas_call x1, Pallas kernels, run_attn_two(): pl.pallas_call(lambda *refs: attn_two_kernel(*refs, count=count), grid=(r...  7.08 us
  transfers between devices with their start and end apart: 37, of which 15 were waited for; matrix products, arithmetic and copies ran while one was open for 10% of the time, Pallas kernels for 15%

profile of v1, /device:TPU:0, one launch (start us, length us, event | category | flops | bytes accessed | tf_op | source)
XLA Modules:
  0.0 341.3 jit_solution(10713339976423457000)
XLA Ops:
  4.8 1.8 pad_maximum_fusion.wb_ref
  6.7 3.0 collective-permute-start.6
  9.9 1.9 collective-permute-start.8
  11.7 24.9 %collective-permute-done.6.refs_5_.wb_ref = bf16[768,768]{1,0:T(8,128)(2,1)} collective-permute-done((bf16[768,768]{1,0:T(8,128)(2,1)S(1)}, bf16[768,768]{1,0:T(8,128)(2,1)}, u32[]{:S(2)}, u32[]{:S(2)}) %collective-permute-start.6) | collective-permute-done | bytes 1179680 | tf_op jit(solution)/shard_map/ppermute | solution.py:495
  37.2 1.9 collective-permute-done
  39.1 2.1 collective-permute-start.1
  41.1 45.2 %collective-permute-done.1 = f32[8]{0:T(128)S(1)} collective-permute-done((f32[8]{0:T(128)S(1)}, f32[8]{0:T(128)S(1)}, u32[]{:S(2)}, u32[]{:S(2)}) %collective-permute-start.1) | collective-permute-done | bytes 64 | tf_op jit(solution)/shard_map/ppermute | solution.py:495
  86.3 1.7 collective-permute-start.2
  88.1 1.8 collective-permute-done.2
  89.9 1.8 collective-permute-start.3
  91.7 1.7 collective-permute-done.3
  93.4 2.8 collective-permute-start.4
  96.2 1.6 collective-permute-done.4
  104.5 4.5 %shard_map.390 = (f32[512,768]{1,0:T(8,128)S(1)}, bf16[512,768]{1,0:T(8,128)(2,1)S(1)}, bf16[6,256,256]{2,1,0:T(8,128)(2,1)S(1)}, bf16[512,768]{1,0:T(8,128)(2,1)S(1)}, bf16[6,256,256]{2,1,0:T(8,128)(2,1)S(1)}) custom-call(bf16[512,768]{1,0:T(8,128)(2,1)S(1)} %get-tuple-element.61.x_ref.refs_1_, bf16[512,768]{1,0:T(8,128)(2,1)S(1)} %copy-done.3, ...), custom_call_target="tpu_custom_call" | custom-call | flops 1610612736 | bytes 10485760 | tf_op jit(solution)/shard_map/pallas_call | solution.py:212
  112.7 7.1 %shard_map.391 = (f32[512,768]{1,0:T(8,128)S(1)}, bf16[512,768]{1,0:T(8,128)(2,1)S(1)}, bf16[8,96,512]{2,1,0:T(8,128)(2,1)S(1)}, bf16[512,768]{1,0:T(8,128)(2,1)...) custom-call(s32[8]{0:T(128)S(1)} %shift-left_add_fusion.refs_0_, ...), custom_call_target="tpu_custom_call" | custom-call | flops 1610612736 | bytes 10485760 | tf_op jit(solution)/shard_map/pallas_call | solution.py:231
  124.7 14.5 %shard_map.393 = (f32[512,768]{1,0:T(8,128)S(1)}, f32[512,768]{1,0:T(8,128)}, bf16[768,768]{1,0:T(8,128)(2,1)}, bf16[768,768]{1,0:T(8,128)(2,1)S(1)}, bf16[768,7...) custom-call(bf16[512,768]{1,0:T(8,128)(2,1)S(1)} %get-tuple-element.63.mid_ref.refs_2_, bf16[768,512]{1,0:T(8,128)(2,1)S(1)} %bitcast.41, ...), custom_call_target="tpu_custom_call" | custom-call | flops 8455716864 | bytes 16777216 | tf_op jit(solution)/shard_map/pallas_call | solution.py:346
  141.7 19.6 %shard_map.394 = (bf16[512,768]{1,0:T(8,128)(2,1)}, f32[512,768]{1,0:T(8,128)}, bf16[512,768]{1,0:T(8,128)(2,1)S(1)}, bf16[8,96,512]{2,1,0:T(8,128)(2,1)S(1)}, f...) custom-call(s32[8]{0:T(128)S(1)} %shift-left_add_fusion.refs_0_, ...), custom_call_target="tpu_custom_call" | custom-call | flops 8455716864 | bytes 16777216 | tf_op jit(solution)/shard_map/pallas_call | solution.py:362
  162.3 1.3 copy-done.24
  167.1 11.8 %shard_map.395 = (f32[512,768]{1,0:T(8,128)S(1)}, bf16[768,768]{1,0:T(8,128)(2,1)S(1)}, bf16[768,768]{1,0:T(8,128)(2,1)S(1)}) custom-call(bf16[512,768]{1,0:T(8,128)(2,1)S(1)} %get-tuple-element.71.gf_ref, bf16[768,512]{1,0:T(8,128)(2,1)S(1)} %bitcast.35, bf16[768,512]{1,0:T(8,128)(2,1)S(1)} %bitcast.39, ...), custom_call_target="tpu_custom_call" | custom-call | flops 3422552064 | bytes 12582912 | tf_op jit(solution)/shard_map/pallas_call | solution.py:471
  180.8 2.8 add_convert_fusion
  183.6 1.7 collective-permute-start.28
  186.5 11.7 %shard_map.396 = (f32[512,768]{1,0:T(8,128)}, f32[8,768]{1,0:T(8,128)S(1)}, bf16[768,768]{1,0:T(8,128)(2,1)}, bf16[768,768]{1,0:T(8,128)(2,1)S(1)}) custom-call(bf16[512,768]{1,0:T(8,128)(2,1)S(1)} %copy-done.37, bf16[768,512]{1,0:T(8,128)(2,1)S(1)} %bitcast.36, bf16[768,512]{1,0:T(8,128)(2,1)S(1)} %bitcast.40, bf16[768,768]{1,0:T(8,128)(2,1)S(1)} %copy-done.15, ...), custom_call_target="tpu_custom_call" | custom-call | flops 3422552064 | bytes 12582912 | tf_op jit(solution)/shard_map/pallas_call | solution.py:481
  198.3 1.4 add_convert_fusion.2
  202.8 1.5 collective-permute-start.22
  205.3 1.8 copy.85
  208.6 1.6 copy.88
  212.9 2.0 convert_add_fusion
  214.9 1.6 collective-permute-start.29
  216.6 21.4 %collective-permute-done.16 = bf16[768,768]{1,0:T(8,128)(2,1)} collective-permute-done((bf16[768,768]{1,0:T(8,128)(2,1)}, bf16[768,768]{1,0:T(8,128)(2,1)}, u32[]{:S(2)}, u32[]{:S(2)}) %collective-permute-start.16) | collective-permute-done | bytes 1179680 | tf_op jit(solution)/shard_map/ppermute | solution.py:495
  238.0 2.2 convert_add_fusion.2
  240.2 1.8 collective-permute-start.17
  242.0 20.6 %collective-permute-done.22 = bf16[768,768]{1,0:T(8,128)(2,1)} collective-permute-done((bf16[768,768]{1,0:T(8,128)(2,1)}, bf16[768,768]{1,0:T(8,128)(2,1)}, u32[]{:S(2)}, u32[]{:S(2)}) %collective-permute-start.22) | collective-permute-done | bytes 1179680 | tf_op jit(solution)/shard_map/ppermute | solution.py:495
  262.6 2.0 convert_add_fusion.1
  264.7 1.8 collective-permute-start.23
  266.6 1.6 collective-permute-start.30
  268.9 10.5 %collective-permute-done.23 = bf16[384,768]{1,0:T(8,128)(2,1)S(1)} collective-permute-done((bf16[384,768]{1,0:T(8,128)(2,1)S(1)}, bf16[384,768]{1,0:T(8,128)(2,1)S(1)}, u32[]{:S(2)}, u32[]{:S(2)}) %collective-permute-start.23) | collective-permute-done | bytes 589856 | tf_op jit(solution)/shard_map/ppermute | solution.py:495
  279.6 1.9 collective-permute-start.24
  282.2 2.6 collective-permute-start.31
  285.3 6.8 %collective-permute-done.24 = bf16[192,768]{1,0:T(8,128)(2,1)S(1)} collective-permute-done((bf16[192,768]{1,0:T(8,128)(2,1)S(1)}, bf16[192,768]{1,0:T(8,128)(2,1)S(1)}, u32[]{:S(2)}, u32[]{:S(2)}) %collective-permute-start.24) | collective-permute-done | bytes 294944 | tf_op jit(solution)/shard_map/ppermute | solution.py:495
  294.0 8.2 %collective-permute-done.19 = bf16[96,768]{1,0:T(8,128)(2,1)S(1)} collective-permute-done((bf16[96,768]{1,0:T(8,128)(2,1)S(1)}, bf16[96,768]{1,0:T(8,128)(2,1)S(1)}, u32[]{:S(2)}, u32[]{:S(2)}) %collective-permute-start.19) | collective-permute-done | bytes 147488 | tf_op jit(solution)/shard_map/ppermute | solution.py:495
  303.6 2.7 multiply_reduce_fusion
  307.0 2.6 multiply_reduce_fusion.1
  309.6 5.3 %stack.41 = f32[8]{0:T(128)S(1)} concatenate(f32[1]{0:T(128)} %bitcast.13, f32[1]{0:T(128)} %bitcast.14, f32[1]{0:T(128)} %bitcast.15, f32[1]{0:T(128)} %bitcast.16, f32[1]{0:T(128)} %bitcast.17, f32[1]{0:T(128)} %bitcast.18, f32[1]{0:T(128)} %bitcast.19, f32[1]{0:T(128)} %bitcast.20), dimensions={0} | concatenate | bytes 64 | tf_op jit(solution)/shard_map/stack | solution.py:611
  316.1 1.6 collective-permute-start.33
  317.7 2.3 collective-permute-done.33
  320.0 1.5 collective-permute-start.34
  321.5 2.3 collective-permute-done.34
  323.9 3.8 %collective-permute-done.35 = f32[8,768]{1,0:T(8,128)S(1)} collective-permute-done((f32[8,768]{1,0:T(8,128)S(1)}, f32[8,768]{1,0:T(8,128)S(1)}, u32[]{:S(2)}, u32[]{:S(2)}) %collective-permute-start.35) | collective-permute-done | bytes 24608 | tf_op jit(solution)/shard_map/ppermute | solution.py:495
  (271 shorter events, 56.6 us)
Async XLA Ops:
  4.8 31.8 %copy-start.79 = (s32[2]{0:T(128)S(1)}, s32[2]{0:T(128)}, u32[]{:S(2)}) copy-start(s32[2]{0:T(128)} %param.24) | copy-start | bytes 28
  4.8 94.7 %copy-start.3 = (bf16[512,768]{1,0:T(8,128)(2,1)S(1)}, bf16[512,768]{1,0:T(8,128)(2,1)}, u32[]{:S(2)}) copy-start(bf16[512,768]{1,0:T(8,128)(2,1)} %rows_ref.3) | copy-start | bytes 2359300
  4.8 94.7 %copy-start.5 = (f32[6,768]{1,0:T(8,128)S(1)}, f32[6,768]{1,0:T(8,128)}, u32[]{:S(2)}) copy-start(f32[6,768]{1,0:T(8,128)} %vec_ref.3) | copy-start | bytes 55300
  4.8 98.9 %copy-start.2 = (bf16[512,768]{1,0:T(8,128)(2,1)S(1)}, bf16[512,768]{1,0:T(8,128)(2,1)}, u32[]{:S(2)}) copy-start(bf16[512,768]{1,0:T(8,128)(2,1)} %refs_13_.1) | copy-start | bytes 2359300
  6.7 29.9 %collective-permute-start.6 = (bf16[768,768]{1,0:T(8,128)(2,1)S(1)}, bf16[768,768]{1,0:T(8,128)(2,1)}, u32[]{:S(2)}, u32[]{:S(2)}) collective-permute-start(bf16[768,768]{1,0:T(8,128)(2,1)S(1)} %pad_maximum_fusion.wb_ref), channel_id=1, source_target_pairs={{0,2},{1,3},{2,0},{3,1},{4,6},{5,7},{6,4},{7,5},{8,10},{9,11},{10,... | collective-permute-start | bytes 3538952 | tf_op jit(solution)/shard_map/ppermute | solution.py:495
  9.7 88.2 %collective-permute-start.5 = (bf16[768,768]{1,0:T(8,128)(2,1)S(1)}, bf16[768,768]{1,0:T(8,128)(2,1)S(1)}, u32[]{:S(2)}, u32[]{:S(2)}) collective-permute-start(bf16[768,768]{1,0:T(8,128)(2,1)S(1)} %pad_maximum_fusion.wb_ref), channel_id=1, source_target_pairs={{0,1},{1,0},{2,3},{3,2},{4,5},{5,4},{6,7},{7,6},{8,9},{9,8},{10,11... | collective-permute-start | bytes 3538952 | tf_op jit(solution)/shard_map/ppermute | solution.py:495
  9.7 92.7 %collective-permute-start.10 = (bf16[768,768]{1,0:T(8,128)(2,1)}, bf16[768,768]{1,0:T(8,128)(2,1)}, u32[]{:S(2)}, u32[]{:S(2)}) collective-permute-start(bf16[768,768]{1,0:T(8,128)(2,1)} %db_ref.1), channel_id=1, source_target_pairs={{0,2},{1,3},{2,0},{3,1},{4,6},{5,7},{6,4},{7,5},{8,10},{9,11},{10,... | collective-permute-start | bytes 3538952 | tf_op jit(solution)/shard_map/ppermute | solution.py:495
  9.9 92.7 %collective-permute-start.8 = (bf16[768,768]{1,0:T(8,128)(2,1)}, bf16[768,768]{1,0:T(8,128)(2,1)}, u32[]{:S(2)}, u32[]{:S(2)}) collective-permute-start(bf16[768,768]{1,0:T(8,128)(2,1)} %ib_ref.1), channel_id=1, source_target_pairs={{0,2},{1,3},{2,0},{3,1},{4,6},{5,7},{6,4},{7,5},{8,10},{9,11},{10,... | collective-permute-start | bytes 3538952 | tf_op jit(solution)/shard_map/ppermute | solution.py:495
  36.6 76.1 %collective-permute-start.7 = (bf16[768,768]{1,0:T(8,128)(2,1)}, bf16[768,768]{1,0:T(8,128)(2,1)}, u32[]{:S(2)}, u32[]{:S(2)}) collective-permute-start(bf16[768,768]{1,0:T(8,128)(2,1)} %collective-permute-done.6.refs_5_.wb_ref), channel_id=1, source_target_pairs={{0,1},{1,0},{2,3},{3,2},{4,5},{5,4},{6,7},{7,6},{8,9},{9,8},{10,11... | collective-permute-start | bytes 3538952 | tf_op jit(solution)/shard_map/ppermute | solution.py:495
  36.7 2.4 collective-permute-start
  39.1 47.3 %collective-permute-start.1 = (f32[8]{0:T(128)S(1)}, f32[8]{0:T(128)S(1)}, u32[]{:S(2)}, u32[]{:S(2)}) collective-permute-start(f32[8]{0:T(128)S(1)} %add.171), channel_id=1, source_target_pairs={{0,2},{1,3},{2,0},{3,1},{4,6},{5,7},{6,4},{7,5},{8,10},{9,11},{10,... | collective-permute-start | bytes 104 | tf_op jit(solution)/shard_map/ppermute | solution.py:495
  86.3 3.5 %collective-permute-start.2 = (f32[8]{0:T(128)S(1)}, f32[8]{0:T(128)S(1)}, u32[]{:S(2)}, u32[]{:S(2)}) collective-permute-start(f32[8]{0:T(128)S(1)} %add.172), channel_id=1, source_target_pairs={{0,4},{4,0},{8,12},{12,8},{16,20},{20,16},{24,28},{28,24},{1,5},{5... | collective-permute-start | bytes 104 | tf_op jit(solution)/shard_map/ppermute | solution.py:495
  89.9 3.5 %collective-permute-start.3 = (f32[8]{0:T(128)S(1)}, f32[8]{0:T(128)S(1)}, u32[]{:S(2)}, u32[]{:S(2)}) collective-permute-start(f32[8]{0:T(128)S(1)} %add.173), channel_id=1, source_target_pairs={{0,8},{4,12},{8,0},{12,4},{16,24},{20,28},{24,16},{28,20},{1,9},{5... | collective-permute-start | bytes 104 | tf_op jit(solution)/shard_map/ppermute | solution.py:495
  93.4 4.4 %collective-permute-start.4 = (f32[8]{0:T(128)S(1)}, f32[8]{0:T(128)S(1)}, u32[]{:S(2)}, u32[]{:S(2)}) collective-permute-start(f32[8]{0:T(128)S(1)} %add.174), channel_id=1, source_target_pairs={{0,16},{4,20},{8,24},{12,28},{16,0},{20,4},{24,8},{28,12},{1,17},{... | collective-permute-start | bytes 104 | tf_op jit(solution)/shard_map/ppermute | solution.py:495
  97.9 26.7 %collective-permute-start.12 = (bf16[768,768]{1,0:T(8,128)(2,1)}, bf16[768,768]{1,0:T(8,128)(2,1)}, u32[]{:S(2)}, u32[]{:S(2)}) collective-permute-start(bf16[768,768]{1,0:T(8,128)(2,1)} %ib_ref.1), channel_id=1, source_target_pairs={{0,1},{1,0},{2,3},{3,2},{4,5},{5,4},{6,7},{7,6},{8,9},{9,8},{10,11... | collective-permute-start | bytes 3538952 | tf_op jit(solution)/shard_map/ppermute | solution.py:495
  99.0 25.6 %collective-permute-start.13 = (bf16[768,768]{1,0:T(8,128)(2,1)}, bf16[768,768]{1,0:T(8,128)(2,1)}, u32[]{:S(2)}, u32[]{:S(2)}) collective-permute-start(bf16[768,768]{1,0:T(8,128)(2,1)} %db_ref.1), channel_id=1, source_target_pairs={{0,1},{1,0},{2,3},{3,2},{4,5},{5,4},{6,7},{7,6},{8,9},{9,8},{10,11... | collective-permute-start | bytes 3538952 | tf_op jit(solution)/shard_map/ppermute | solution.py:495
  102.4 37.8 %collective-permute-start.11 = (bf16[768,768]{1,0:T(8,128)(2,1)}, bf16[768,768]{1,0:T(8,128)(2,1)S(1)}, u32[]{:S(2)}, u32[]{:S(2)}) collective-permute-start(bf16[768,768]{1,0:T(8,128)(2,1)} %collective-permute-done.10.refs_9_), channel_id=1, source_target_pairs={{0,1},{1,0},{2,3},{3,2},{4,5},{5,4},{6,7},{7,6},{8,9},{9,8},{10,11... | collective-permute-start | bytes 3538952 | tf_op jit(solution)/shard_map/ppermute | solution.py:495
  102.5 37.8 %collective-permute-start.9 = (bf16[768,768]{1,0:T(8,128)(2,1)}, bf16[768,768]{1,0:T(8,128)(2,1)S(1)}, u32[]{:S(2)}, u32[]{:S(2)}) collective-permute-start(bf16[768,768]{1,0:T(8,128)(2,1)} %collective-permute-done.8.refs_8_), channel_id=1, source_target_pairs={{0,1},{1,0},{2,3},{3,2},{4,5},{5,4},{6,7},{7,6},{8,9},{9,8},{10,11... | collective-permute-start | bytes 3538952 | tf_op jit(solution)/shard_map/ppermute | solution.py:495
  104.5 20.1 %copy-start.21 = (bf16[512,768]{1,0:T(8,128)(2,1)}, bf16[512,768]{1,0:T(8,128)(2,1)S(1)}, u32[]{:S(2)}) copy-start(bf16[512,768]{1,0:T(8,128)(2,1)S(1)} %get-tuple-element.65.g_ref.refs_4_) | copy-start | bytes 2359300
  140.3 21.0 %copy-start.16 = (bf16[768,768]{1,0:T(8,128)(2,1)}, bf16[768,768]{1,0:T(8,128)(2,1)S(1)}, u32[]{:S(2)}) copy-start(bf16[768,768]{1,0:T(8,128)(2,1)S(1)} %get-tuple-element.94) | copy-start | bytes 3538948
  141.7 20.6 %copy-start.19 = (bf16[8,96,512]{2,1,0:T(8,128)(2,1)S(1)}, bf16[8,96,512]{2,1,0:T(8,128)(2,1)}, u32[]{:S(2)}) copy-start(bf16[8,96,512]{2,1,0:T(8,128)(2,1)} %copy-done.18) | copy-start | bytes 2359300
  141.7 20.6 %copy-start.40 = (bf16[512,768]{1,0:T(8,128)(2,1)S(1)}, bf16[512,768]{1,0:T(8,128)(2,1)}, u32[]{:S(2)}) copy-start(bf16[512,768]{1,0:T(8,128)(2,1)} %copy-done.39) | copy-start | bytes 2359300
  162.2 17.5 %collective-permute-start.27 = (bf16[768,768]{1,0:T(8,128)(2,1)}, bf16[768,768]{1,0:T(8,128)(2,1)S(1)}, u32[]{:S(2)}, u32[]{:S(2)}) collective-permute-start(bf16[768,768]{1,0:T(8,128)(2,1)} %get-tuple-element.96), channel_id=1, source_target_pairs={{0,1},{1,0},{2,3},{3,2},{4,5},{5,4},{6,7},{7,6},{8,9},{9,8},{10,11... | collective-permute-start | bytes 3538952 | tf_op jit(solution)/shard_map/ppermute | solution.py:495
  178.9 19.3 %collective-permute-start.15 = (bf16[768,768]{1,0:T(8,128)(2,1)S(1)}, bf16[768,768]{1,0:T(8,128)(2,1)S(1)}, u32[]{:S(2)}, u32[]{:S(2)}) collective-permute-start(bf16[768,768]{1,0:T(8,128)(2,1)S(1)} %get-tuple-element.88), channel_id=1, source_target_pairs={{0,1},{1,0},{2,3},{3,2},{4,5},{5,4},{6,7},{7,6},{8,9},{9,8},{10,11... | collective-permute-start | bytes 3538952 | tf_op jit(solution)/shard_map/ppermute | solution.py:495
  179.2 20.7 %collective-permute-start.21 = (bf16[768,768]{1,0:T(8,128)(2,1)}, bf16[768,768]{1,0:T(8,128)(2,1)S(1)}, u32[]{:S(2)}, u32[]{:S(2)}) collective-permute-start(bf16[768,768]{1,0:T(8,128)(2,1)} %get-tuple-element.92), channel_id=1, source_target_pairs={{0,1},{1,0},{2,3},{3,2},{4,5},{5,4},{6,7},{7,6},{8,9},{9,8},{10,11... | collective-permute-start | bytes 3538952 | tf_op jit(solution)/shard_map/ppermute | solution.py:495
  179.5 22.2 %collective-permute-start.26 = (bf16[768,768]{1,0:T(8,128)(2,1)S(1)}, bf16[768,768]{1,0:T(8,128)(2,1)S(1)}, u32[]{:S(2)}, u32[]{:S(2)}) collective-permute-start(bf16[768,768]{1,0:T(8,128)(2,1)S(1)} %copy-done.17), channel_id=1, source_target_pairs={{0,1},{1,0},{2,3},{3,2},{4,5},{5,4},{6,7},{7,6},{8,9},{9,8},{10,11... | collective-permute-start | bytes 3538952 | tf_op jit(solution)/shard_map/ppermute | solution.py:495
  183.6 29.3 %collective-permute-start.28 = (bf16[768,768]{1,0:T(8,128)(2,1)}, bf16[768,768]{1,0:T(8,128)(2,1)}, u32[]{:S(2)}, u32[]{:S(2)}) collective-permute-start(bf16[768,768]{1,0:T(8,128)(2,1)} %add_convert_fusion), channel_id=1, source_target_pairs={{0,2},{1,3},{2,0},{3,1},{4,6},{5,7},{6,4},{7,5},{8,10},{9,11},{10,... | collective-permute-start | bytes 3538952 | tf_op jit(solution)/shard_map/ppermute | solution.py:495
  198.3 18.3 %collective-permute-start.14 = (bf16[768,768]{1,0:T(8,128)(2,1)}, bf16[768,768]{1,0:T(8,128)(2,1)}, u32[]{:S(2)}, u32[]{:S(2)}) collective-permute-start(bf16[768,768]{1,0:T(8,128)(2,1)} %get-tuple-element.86), channel_id=1, source_target_pairs={{0,1},{1,0},{2,3},{3,2},{4,5},{5,4},{6,7},{7,6},{8,9},{9,8},{10,11... | collective-permute-start | bytes 3538952 | tf_op jit(solution)/shard_map/ppermute | solution.py:495
  199.7 38.3 %collective-permute-start.16 = (bf16[768,768]{1,0:T(8,128)(2,1)}, bf16[768,768]{1,0:T(8,128)(2,1)}, u32[]{:S(2)}, u32[]{:S(2)}) collective-permute-start(bf16[768,768]{1,0:T(8,128)(2,1)} %add_convert_fusion.2), channel_id=1, source_target_pairs={{0,2},{1,3},{2,0},{3,1},{4,6},{5,7},{6,4},{7,5},{8,10},{9,11},{10,... | collective-permute-start | bytes 3538952 | tf_op jit(solution)/shard_map/ppermute | solution.py:495
  200.0 42.0 %collective-permute-start.20 = (bf16[768,768]{1,0:T(8,128)(2,1)}, bf16[768,768]{1,0:T(8,128)(2,1)}, u32[]{:S(2)}, u32[]{:S(2)}) collective-permute-start(bf16[768,768]{1,0:T(8,128)(2,1)} %get-tuple-element.90), channel_id=1, source_target_pairs={{0,1},{1,0},{2,3},{3,2},{4,5},{5,4},{6,7},{7,6},{8,9},{9,8},{10,11... | collective-permute-start | bytes 3538952 | tf_op jit(solution)/shard_map/ppermute | solution.py:495
  202.8 59.8 %collective-permute-start.22 = (bf16[768,768]{1,0:T(8,128)(2,1)}, bf16[768,768]{1,0:T(8,128)(2,1)}, u32[]{:S(2)}, u32[]{:S(2)}) collective-permute-start(bf16[768,768]{1,0:T(8,128)(2,1)} %add_convert_fusion.1), channel_id=1, source_target_pairs={{0,2},{1,3},{2,0},{3,1},{4,6},{5,7},{6,4},{7,5},{8,10},{9,11},{10,... | collective-permute-start | bytes 3538952 | tf_op jit(solution)/shard_map/ppermute | solution.py:495
  214.9 23.1 %copy-start.1 = (bf16[768,768]{1,0:T(8,128)(2,1)S(1)}, bf16[768,768]{1,0:T(8,128)(2,1)}, u32[]{:S(2)}) copy-start(bf16[768,768]{1,0:T(8,128)(2,1)} %copy-done) | copy-start | bytes 3538948
  214.9 51.5 %collective-permute-start.29 = (bf16[384,768]{1,0:T(8,128)(2,1)S(1)}, bf16[384,768]{1,0:T(8,128)(2,1)S(1)}, u32[]{:S(2)}, u32[]{:S(2)}) collective-permute-start(bf16[384,768]{1,0:T(8,128)(2,1)S(1)} %slice.195), channel_id=1, source_target_pairs={{0,4},{4,0},{8,12},{12,8},{16,20},{20,16},{24,28},{28,24},{1,5},{5... | collective-permute-start | bytes 1769480 | tf_op jit(solution)/shard_map/ppermute | solution.py:495
  240.2 28.1 %collective-permute-start.17 = (bf16[384,768]{1,0:T(8,128)(2,1)S(1)}, bf16[384,768]{1,0:T(8,128)(2,1)S(1)}, u32[]{:S(2)}, u32[]{:S(2)}) collective-permute-start(bf16[384,768]{1,0:T(8,128)(2,1)S(1)} %slice.197), channel_id=1, source_target_pairs={{0,4},{4,0},{8,12},{12,8},{16,20},{20,16},{24,28},{28,24},{1,5},{5... | collective-permute-start | bytes 1769480 | tf_op jit(solution)/shard_map/ppermute | solution.py:495
  264.7 14.8 %collective-permute-start.23 = (bf16[384,768]{1,0:T(8,128)(2,1)S(1)}, bf16[384,768]{1,0:T(8,128)(2,1)S(1)}, u32[]{:S(2)}, u32[]{:S(2)}) collective-permute-start(bf16[384,768]{1,0:T(8,128)(2,1)S(1)} %slice.196), channel_id=1, source_target_pairs={{0,4},{4,0},{8,12},{12,8},{16,20},{20,16},{24,28},{28,24},{1,5},{5... | collective-permute-start | bytes 1769480 | tf_op jit(solution)/shard_map/ppermute | solution.py:495
  266.6 14.9 %collective-permute-start.30 = (bf16[192,768]{1,0:T(8,128)(2,1)S(1)}, bf16[192,768]{1,0:T(8,128)(2,1)S(1)}, u32[]{:S(2)}, u32[]{:S(2)}) collective-permute-start(bf16[192,768]{1,0:T(8,128)(2,1)S(1)} %slice.198), channel_id=1, source_target_pairs={{0,8},{4,12},{8,0},{12,4},{16,24},{20,28},{24,16},{28,20},{1,9},{5... | collective-permute-start | bytes 884744 | tf_op jit(solution)/shard_map/ppermute | solution.py:495
  268.4 16.4 %collective-permute-start.18 = (bf16[192,768]{1,0:T(8,128)(2,1)S(1)}, bf16[192,768]{1,0:T(8,128)(2,1)S(1)}, u32[]{:S(2)}, u32[]{:S(2)}) collective-permute-start(bf16[192,768]{1,0:T(8,128)(2,1)S(1)} %slice.200), channel_id=1, source_target_pairs={{0,8},{4,12},{8,0},{12,4},{16,24},{20,28},{24,16},{28,20},{1,9},{5... | collective-permute-start | bytes 884744 | tf_op jit(solution)/shard_map/ppermute | solution.py:495
  279.6 12.5 %collective-permute-start.24 = (bf16[192,768]{1,0:T(8,128)(2,1)S(1)}, bf16[192,768]{1,0:T(8,128)(2,1)S(1)}, u32[]{:S(2)}, u32[]{:S(2)}) collective-permute-start(bf16[192,768]{1,0:T(8,128)(2,1)S(1)} %slice.199), channel_id=1, source_target_pairs={{0,8},{4,12},{8,0},{12,4},{16,24},{20,28},{24,16},{28,20},{1,9},{5... | collective-permute-start | bytes 884744 | tf_op jit(solution)/shard_map/ppermute | solution.py:495
  282.2 21.2 %collective-permute-start.31 = (bf16[96,768]{1,0:T(8,128)(2,1)}, bf16[96,768]{1,0:T(8,128)(2,1)}, u32[]{:S(2)}, u32[]{:S(2)}) collective-permute-start(bf16[96,768]{1,0:T(8,128)(2,1)} %slice.201), channel_id=1, source_target_pairs={{0,16},{4,20},{8,24},{12,28},{16,0},{20,4},{24,8},{28,12},{1,17},{... | collective-permute-start | bytes 442376 | tf_op jit(solution)/shard_map/ppermute | solution.py:495
  284.9 17.3 %collective-permute-start.19 = (bf16[96,768]{1,0:T(8,128)(2,1)S(1)}, bf16[96,768]{1,0:T(8,128)(2,1)S(1)}, u32[]{:S(2)}, u32[]{:S(2)}) collective-permute-start(bf16[96,768]{1,0:T(8,128)(2,1)S(1)} %slice.203), channel_id=1, source_target_pairs={{0,16},{4,20},{8,24},{12,28},{16,0},{20,4},{24,8},{28,12},{1,17},{... | collective-permute-start | bytes 442376 | tf_op jit(solution)/shard_map/ppermute | solution.py:495
  292.8 14.1 %collective-permute-start.25 = (bf16[96,768]{1,0:T(8,128)(2,1)}, bf16[96,768]{1,0:T(8,128)(2,1)}, u32[]{:S(2)}, u32[]{:S(2)}) collective-permute-start(bf16[96,768]{1,0:T(8,128)(2,1)} %slice.202), channel_id=1, source_target_pairs={{0,16},{4,20},{8,24},{12,28},{16,0},{20,4},{24,8},{28,12},{1,17},{... | collective-permute-start | bytes 442376 | tf_op jit(solution)/shard_map/ppermute | solution.py:495
  306.2 33.3 %copy-start.58 = (f32[768,96]{0,1:T(8,128)}, f32[768,96]{0,1:T(8,128)S(1)}, u32[]{:S(2)}) copy-start(f32[768,96]{0,1:T(8,128)S(1)} %get-tuple-element.182) | copy-start | bytes 884740
  309.6 30.8 %copy-start.60 = (f32[96,768]{1,0:T(8,128)}, f32[96,768]{1,0:T(8,128)S(1)}, u32[]{:S(2)}) copy-start(f32[96,768]{1,0:T(8,128)S(1)} %get-tuple-element.185) | copy-start | bytes 884740
  314.9 1.3 collective-permute-start.32
  316.1 3.9 %collective-permute-start.33 = (f32[8,768]{1,0:T(8,128)S(1)}, f32[8,768]{1,0:T(8,128)S(1)}, u32[]{:S(2)}, u32[]{:S(2)}) collective-permute-start(f32[8,768]{1,0:T(8,128)S(1)} %fusion.6), channel_id=1, source_target_pairs={{0,2},{1,3},{2,0},{3,1},{4,6},{5,7},{6,4},{7,5},{8,10},{9,11},{10,... | collective-permute-start | bytes 73736 | tf_op jit(solution)/shard_map/ppermute | solution.py:495
  320.0 3.8 %collective-permute-start.34 = (f32[8,768]{1,0:T(8,128)S(1)}, f32[8,768]{1,0:T(8,128)S(1)}, u32[]{:S(2)}, u32[]{:S(2)}) collective-permute-start(f32[8,768]{1,0:T(8,128)S(1)} %add.215), channel_id=1, source_target_pairs={{0,4},{4,0},{8,12},{12,8},{16,20},{20,16},{24,28},{28,24},{1,5},{5... | collective-permute-start | bytes 73736 | tf_op jit(solution)/shard_map/ppermute | solution.py:495
  323.9 3.8 %collective-permute-start.35 = (f32[8,768]{1,0:T(8,128)S(1)}, f32[8,768]{1,0:T(8,128)S(1)}, u32[]{:S(2)}, u32[]{:S(2)}) collective-permute-start(f32[8,768]{1,0:T(8,128)S(1)} %add.216), channel_id=1, source_target_pairs={{0,8},{4,12},{8,0},{12,4},{16,24},{20,28},{24,16},{28,20},{1,9},{5... | collective-permute-start | bytes 73736 | tf_op jit(solution)/shard_map/ppermute | solution.py:495
  327.7 5.3 %collective-permute-start.36 = (f32[8,768]{1,0:T(8,128)S(1)}, f32[8,768]{1,0:T(8,128)S(1)}, u32[]{:S(2)}, u32[]{:S(2)}) collective-permute-start(f32[8,768]{1,0:T(8,128)S(1)} %add.217), channel_id=1, source_target_pairs={{0,16},{4,20},{8,24},{12,28},{16,0},{20,4},{24,8},{28,12},{1,17},{... | collective-permute-start | bytes 73736 | tf_op jit(solution)/shard_map/ppermute | solution.py:495
  (69 other events, 396.6 us)

commit v2 on v1

v2 whole, which is shorter than its diff:
```python
import math

import jax
import jax.numpy as jnp
from jax import lax
from jax.experimental import pallas as pl
from jax.experimental.pallas import tpu as pltpu
from jax.sharding import PartitionSpec as P

HEAD_DIM = 64
PATCHES = 256
GROUPS = 8
STEP = 5

NORM_EPS = 1e-06
ADAM_EPS = 1e-06
MOMENT_DECAY = 0.5
LEARN_RATE = 0.5
WEIGHT_DECAY = 0.01
SCALE = HEAD_DIM ** (-0.5)

F32 = jnp.float32
BF16 = jnp.bfloat16
MB = 1024 * 1024
BIG = 16


def mm(left, right):
    return jnp.dot(left, right, preferred_element_type=F32)


def mm_nt(left, right):
    return lax.dot_general(left, right, (((1,), (1,)), ((), ())), preferred_element_type=F32)


def mm_tn(left, right):
    return lax.dot_general(left, right, (((0,), (0,)), ((), ())), preferred_element_type=F32)


def layer_stats(values):
    center = values - jnp.mean(values, axis=-1, keepdims=True)
    inverse = lax.rsqrt(jnp.mean(center * center, axis=-1, keepdims=True) + NORM_EPS)
    return center * inverse, inverse


def norm_back(grad_normed, normed, inverse):
    return inverse * (
        grad_normed
        - jnp.mean(grad_normed, axis=-1, keepdims=True)
        - normed * jnp.mean(grad_normed * normed, axis=-1, keepdims=True)
    )


def gelu_pair(t):
    size = jnp.abs(t) * (2.0**-0.5)
    k = 1.0 / (1.0 + 0.3275911 * size)
    bell = jnp.exp(-size * size)
    poly = k * (
        0.254829592
        + k * (-0.284496736 + k * (1.421413741 + k * (-1.453152027 + k * 1.061405429)))
    )
    tail = 0.5 * poly * bell
    cdf = jnp.where(t < 0, tail, 1.0 - tail)
    return t * cdf, cdf + t * bell * (1.0 / math.sqrt(2.0 * math.pi))


def put_turned(out_ref, value, pos_ref, count, start):
    turned = value.T
    part = turned.shape[0] // count
    width = turned.shape[1]
    if len(out_ref.shape) == 2:
        out_ref[:, start : start + width] = turned
        return
    for j in range(count):
        out_ref[pos_ref[j], :, start : start + width] = turned[j * part : (j + 1) * part]


def turned_shape(width, rows, count):
    part = width // count
    if part % 16 == 0:
        return (count, part, rows)
    return (width, rows)


def turned_order(turned, pos, count):
    width = turned.shape[0] if turned.ndim == 2 else turned.shape[0] * turned.shape[1]
    rows = turned.shape[-1]
    if turned.ndim == 2:
        shaped = turned.reshape(count, width // count, rows)
        turned = jnp.zeros_like(shaped).at[pos].set(shaped)
    return turned.reshape(width, rows)


def params(limit, **more):
    return pltpu.CompilerParams(vmem_limit_bytes=limit * MB, **more)


def full(shape):
    return pl.BlockSpec(shape, lambda *_: (0,) * len(shape), pipeline_mode=pl.Buffered(1))


SMEM = pl.BlockSpec(memory_space=pltpu.SMEM)


def start_kernel(pos_ref, pos2_ref, rows_ref, vec_ref, x_ref, xt_ref, xt2_ref, *, count):
    width, rows = rows_ref.shape[1], rows_ref.shape[0]
    for start in range(0, rows, PATCHES):
        normed, _ = layer_stats(rows_ref[start : start + PATCHES].astype(F32))
        low = (normed * vec_ref[0:1] + vec_ref[1:2]).astype(BF16)
        x_ref[start : start + PATCHES] = low
        put_turned(xt_ref, low, pos_ref, count, start)
        put_turned(xt2_ref, low, pos2_ref, count, start)


def run_start(pos, pos2, rows, vectors, count):
    r, d = rows.shape
    return pl.pallas_call(
        lambda *refs: start_kernel(*refs, count=count),
        out_shape=(
            jax.ShapeDtypeStruct((r, d), BF16),
            jax.ShapeDtypeStruct(turned_shape(d, r, count), BF16),
            jax.ShapeDtypeStruct(turned_shape(d, r, count), BF16),
        ),
        in_specs=[SMEM, SMEM, pl.BlockSpec(memory_space=pltpu.VMEM), pl.BlockSpec(memory_space=pltpu.VMEM)],
        compiler_params=params(BIG),
    )(pos, pos2, rows, vectors)


def gout_kernel(pos_ref, weight_ref, cot_ref, g_ref, gt_ref, *, count):
    rows = cot_ref.shape[0]
    for index in range(rows // PATCHES):
        start = index * PATCHES
        low = (cot_ref[start : start + PATCHES].astype(F32) * weight_ref[index]).astype(BF16)
        g_ref[start : start + PATCHES] = low
        put_turned(gt_ref, low, pos_ref, count, start)


def run_gout(pos, weight, cot, count):
    r, d = cot.shape
    return pl.pallas_call(
        lambda *refs: gout_kernel(*refs, count=count),
        out_shape=(
            jax.ShapeDtypeStruct((r, d), BF16),
            jax.ShapeDtypeStruct(turned_shape(d, r, count), BF16),
        ),
        in_specs=[SMEM, SMEM, pl.BlockSpec(memory_space=pltpu.VMEM)],
        compiler_params=params(BIG),
    )(pos, weight, cot)


def attend_shard(x, w_ref, saved_ref, probs_ref):
    cols = w_ref.shape[0] // 4
    qkv = mm_nt(x, w_ref[: 3 * cols]).astype(BF16)
    saved_ref[:, : 3 * cols] = qkv
    mixed = []
    for h in range(cols // HEAD_DIM):
        at = h * HEAD_DIM
        q = qkv[:, at : at + HEAD_DIM] * SCALE
        k = qkv[:, cols + at : cols + at + HEAD_DIM]
        v = qkv[:, 2 * cols + at : 2 * cols + at + HEAD_DIM]
        scores = mm_nt(q, k)
        expo = jnp.exp(scores - jnp.max(scores, axis=-1, keepdims=True))
        probs = (expo * (1.0 / jnp.sum(expo, axis=-1, keepdims=True))).astype(BF16)
        probs_ref[h] = probs
        mixed.append(mm(probs, v).astype(BF16))
    mixed = jnp.concatenate(mixed, axis=1)
    saved_ref[:, 3 * cols :] = mixed
    return mm(mixed, w_ref[3 * cols :])


def attn_one_kernel(x_ref, rows_ref, vec_ref, wa_ref, wb_ref, acc_ref, sa_ref, pa_ref, sb_ref, pb_ref):
    x = x_ref[...]
    term = attend_shard(x, wa_ref, sa_ref, pa_ref)
    term += attend_shard(x, wb_ref, sb_ref, pb_ref)
    acc_ref[...] = rows_ref[...].astype(F32) + term + vec_ref[4:5]


def join_halves(low_ref, own_ref, other_ref, whole_ref):
    half = own_ref.shape[0]

    @pl.when(low_ref[0] == 0)
    def _():
        whole_ref[:half] = own_ref[...]
        whole_ref[half:] = other_ref[...]

    @pl.when(low_ref[0] != 0)
    def _():
        whole_ref[:half] = other_ref[...]
        whole_ref[half:] = own_ref[...]


def join_pair(low_ref, halves, wholes):
    @pl.when(pl.program_id(0) == 0)
    def _():
        for (own, other), whole in zip(halves, wholes):
            join_halves(low_ref, own, other, whole)


def attn_two_kernel(
    pos_ref, low_ref, x_ref, acc_ref, vec_ref, ha_ref, ia_ref, hb_ref, ib_ref,
    first_ref, mid_ref, midt_ref, sa_ref, pa_ref, sb_ref, pb_ref, wa_ref, wb_ref, *, count,
):
    join_pair(low_ref, ((ha_ref, ia_ref), (hb_ref, ib_ref)), (wa_ref, wb_ref))
    x = x_ref[...]
    term = attend_shard(x, wa_ref, sa_ref, pa_ref)
    term += attend_shard(x, wb_ref, sb_ref, pb_ref)
    first = acc_ref[...] + term
    first_ref[...] = first
    normed, _ = layer_stats(first)
    low = (normed * vec_ref[2:3] + vec_ref[3:4]).astype(BF16)
    mid_ref[...] = low
    put_turned(midt_ref, low, pos_ref, count, 0)


def image_block(d):
    return pl.BlockSpec((PATCHES, d), lambda i: (i, 0))


def saved_outputs(r, d, heads):
    images = r // PATCHES
    shapes = (
        jax.ShapeDtypeStruct((r, d), BF16),
        jax.ShapeDtypeStruct((images * heads, PATCHES, PATCHES), BF16),
    )
    specs = [image_block(d), pl.BlockSpec((heads, PATCHES, PATCHES), lambda i: (i, 0, 0))]
    return shapes, specs


def cost(micros):
    return pl.CostEstimate(flops=int(micros * 1e9), bytes_accessed=int(micros * 3e6), transcendentals=0)


def run_attn_one(x, rows, vectors, wa, wb):
    r, d = x.shape
    heads = d // 4 // HEAD_DIM
    shapes, specs = saved_outputs(r, d, heads)
    return pl.pallas_call(
        attn_one_kernel,
        grid=(r // PATCHES,),
        out_shape=(jax.ShapeDtypeStruct((r, d), F32),) + shapes * 2,
        in_specs=[image_block(d), image_block(d), full(vectors.shape), full((d, d)), full((d, d))],
        out_specs=[image_block(d)] + specs * 2,
        compiler_params=params(BIG),
        cost_estimate=cost(7),
    )(x, rows, vectors, wa, wb)


def run_attn_two(pos, low, x, acc, vectors, wa, wb, count):
    r, d = x.shape
    heads = d // 4 // HEAD_DIM
    shapes, specs = saved_outputs(r, d, heads)
    tshape = turned_shape(d, r, count)
    tspec = pl.BlockSpec(
        tshape[:-1] + (PATCHES,), lambda i: (0,) * (len(tshape) - 1) + (i,)
    )
    return pl.pallas_call(
        lambda *refs: attn_two_kernel(*refs, count=count),
        grid=(r // PATCHES,),
        out_shape=(
            jax.ShapeDtypeStruct((r, d), F32),
            jax.ShapeDtypeStruct((r, d), BF16),
            jax.ShapeDtypeStruct(tshape, BF16),
        )
        + shapes * 2,
        in_specs=[SMEM, SMEM, image_block(d), image_block(d), full(vectors.shape)]
        + [full((d // 2, d))] * 4,
        out_specs=[image_block(d), image_block(d), tspec] + specs * 2,
        scratch_shapes=[pltpu.VMEM((d, d), BF16)] * 2,
        compiler_params=params(BIG),
        cost_estimate=cost(7),
    )(pos, low, x, acc, vectors, *wa, *wb)


TILES = 3


def ffn_tile(mid_ref, midt_ref, g_ref, gt_ref, w_in, w_down, gi_ref, gd_ref, y_ref, dm_ref):
    pre = mm(mid_ref[...], w_in)
    dact = mm_nt(g_ref[...], w_down)
    activ, slope = gelu_pair(pre)
    activ = activ.astype(BF16)
    dpre = (dact * slope).astype(BF16)
    y_ref[...] += mm(activ, w_down)
    dm_ref[...] += mm_nt(dpre, w_in)
    gd_ref[...] = mm(gt_ref[...], activ).astype(BF16)
    gi_ref[...] = mm(midt_ref[...], dpre).astype(BF16)


def ffn_one_kernel(
    mid_ref, midt_ref, g_ref, gt_ref, ia_ref, da_ref, ib_ref, db_ref,
    y_ref, dm_ref, gia_ref, gda_ref, gib_ref, gdb_ref,
):
    step = pl.program_id(0)

    @pl.when(step == 0)
    def _():
        y_ref[...] = jnp.zeros_like(y_ref)
        dm_ref[...] = jnp.zeros_like(dm_ref)

    @pl.when(step < TILES)
    def _():
        ffn_tile(mid_ref, midt_ref, g_ref, gt_ref, ia_ref[...], da_ref[...], gia_ref, gda_ref, y_ref, dm_ref)

    @pl.when(step >= TILES)
    def _():
        ffn_tile(mid_ref, midt_ref, g_ref, gt_ref, ib_ref[...], db_ref[...], gib_ref, gdb_ref, y_ref, dm_ref)


def joined(low_ref, own_ref, other_ref, axis):
    own, other = own_ref[...], other_ref[...]
    return jnp.where(
        low_ref[0] == 0,
        jnp.concatenate([own, other], axis=axis),
        jnp.concatenate([other, own], axis=axis),
    )


def ffn_two_kernel(
    pos_ref, low_ref, weight_ref, mid_ref, midt_ref, g_ref, gt_ref,
    ia_ref, ja_ref, da_ref, ea_ref, ib_ref, jb_ref, db_ref, eb_ref,
    y_in_ref, dm_in_ref, first_ref, cot_ref, vec_ref,
    out_ref, gf_ref, gfl_ref, gft_ref, sums_ref, gia_ref, gda_ref, gib_ref, gdb_ref,
    y_ref, dm_ref, *, count,
):
    step = pl.program_id(0)

    @pl.when(step == 0)
    def _():
        y_ref[...] = y_in_ref[...]
        dm_ref[...] = dm_in_ref[...]

    @pl.when(step < TILES)
    def _():
        w_in, w_down = joined(low_ref, ia_ref, ja_ref, 0), joined(low_ref, da_ref, ea_ref, 1)
        ffn_tile(mid_ref, midt_ref, g_ref, gt_ref, w_in, w_down, gia_ref, gda_ref, y_ref, dm_ref)

    @pl.when(step >= TILES)
    def _():
        w_in, w_down = joined(low_ref, ib_ref, jb_ref, 0), joined(low_ref, db_ref, eb_ref, 1)
        ffn_tile(mid_ref, midt_ref, g_ref, gt_ref, w_in, w_down, gib_ref, gdb_ref, y_ref, dm_ref)

    @pl.when(step == pl.num_programs(0) - 1)
    def _():
        rows = first_ref.shape[0]
        sums = [0.0, 0.0, 0.0, 0.0]
        chunk = 128
        for start in range(0, rows, chunk):
            here = slice(start, start + chunk)
            first = first_ref[here]
            normed, inverse = layer_stats(first)
            out_ref[here] = (first + y_ref[here] + vec_ref[5:6]).astype(BF16)
            dmid = dm_ref[here]
            gout = cot_ref[here].astype(F32) * weight_ref[start // PATCHES]
            gfirst = gout + norm_back(dmid * vec_ref[2:3], normed, inverse)
            gf_ref[here] = gfirst
            low = gfirst.astype(BF16)
            gfl_ref[here] = low
            put_turned(gft_ref, low, pos_ref, count, start)
            for index, term in enumerate((dmid * normed, dmid, gfirst, gout)):
                sums[index] += jnp.sum(term, axis=0, keepdims=True)
        sums_ref[...] = jnp.concatenate(sums + sums, axis=0)


def ffn_specs(d, parts):
    tile = d // TILES
    cols = lambda f: pl.BlockSpec((d, tile), lambda i: (0, f(i)))
    w_in = lambda f: pl.BlockSpec((d // parts, tile), lambda i: (0, f(i)))
    w_down = lambda f: pl.BlockSpec((tile, d // parts), lambda i: (f(i), 0))
    fa = lambda i: jnp.minimum(i, TILES - 1)
    fb = lambda i: jnp.maximum(i - TILES, 0)
    weights = [kind(f) for f in (fa, fb) for kind in (w_in, w_down) for _ in range(parts)]
    return weights, [cols(fa), cols(fa), cols(fb), cols(fb)]


def run_ffn_one(mid, midt, g, gt, wa, wb):
    r, d = mid.shape
    w_specs, g_specs = ffn_specs(d, 1)
    grad = jax.ShapeDtypeStruct((d, d), BF16)
    return pl.pallas_call(
        ffn_one_kernel,
        grid=(2 * TILES,),
        out_shape=(jax.ShapeDtypeStruct((r, d), F32),) * 2 + (grad,) * 4,
        in_specs=[full((r, d)), full((d, r)), full((r, d)), full((d, r))] + w_specs,
        out_specs=[full((r, d)), full((r, d))] + g_specs,
        compiler_params=params(BIG),
        cost_estimate=cost(13),
    )(mid, midt, g, gt, *wa, *wb)


def run_ffn_two(pos, low, weight, mid, midt, g, gt, wa, wb, y, dm, first, cot, vectors, count):
    r, d = mid.shape
    w_specs, g_specs = ffn_specs(d, 2)
    grad = jax.ShapeDtypeStruct((d, d), BF16)
    tshape = turned_shape(d, r, count)
    return pl.pallas_call(
        lambda *refs: ffn_two_kernel(*refs, count=count),
        grid=(2 * TILES,),
        out_shape=(
            jax.ShapeDtypeStruct((r, d), BF16),
            jax.ShapeDtypeStruct((r, d), F32),
            jax.ShapeDtypeStruct((r, d), BF16),
            jax.ShapeDtypeStruct(tshape, BF16),
            jax.ShapeDtypeStruct((8, d), F32),
        )
        + (grad,) * 4,
        in_specs=[SMEM, SMEM, SMEM, full((r, d)), full((d, r)), full((r, d)), full((d, r))]
        + w_specs
        + [full((r, d))] * 4
        + [full(vectors.shape)],
        out_specs=[full((r, d)), full((r, d)), full((r, d)), full(tshape), full((8, d))] + g_specs,
        scratch_shapes=[pltpu.VMEM((r, d), F32), pltpu.VMEM((r, d), F32)],
        compiler_params=params(BIG),
        cost_estimate=cost(13),
    )(pos, low, weight, mid, midt, g, gt, *wa, *wb, y, dm, first, cot, vectors)


def attend_back_shard(gf, w_ref, saved_ref, probs_ref, keep_ref):
    cols = w_ref.shape[0] // 4
    start = pl.multiple_of(pl.program_id(0) * PATCHES, PATCHES)
    dmix = mm_nt(gf, w_ref[3 * cols :]).astype(BF16)
    dq, dk, dv = [], [], []
    for h in range(cols // HEAD_DIM):
        at = h * HEAD_DIM
        q = saved_ref[:, at : at + HEAD_DIM]
        k = saved_ref[:, cols + at : cols + at + HEAD_DIM]
        v = saved_ref[:, 2 * cols + at : 2 * cols + at + HEAD_DIM]
        do = dmix[:, at : at + HEAD_DIM]
        probs = probs_ref[h]
        dv.append(mm_tn(probs, do).astype(BF16))
        dp = mm_nt(do, v)
        wide = probs.astype(F32)
        ds = (SCALE * wide * (dp - jnp.sum(wide * dp, axis=-1, keepdims=True))).astype(BF16)
        dq.append(mm(ds, k).astype(BF16))
        dk.append(mm_tn(ds, q).astype(BF16))
    dqkv = jnp.concatenate(dq + dk + dv, axis=1)
    keep_ref[pl.ds(start, PATCHES), : 3 * cols] = dqkv
    keep_ref[pl.ds(start, PATCHES), 3 * cols :] = saved_ref[:, 3 * cols :]
    return mm(dqkv, w_ref[: 3 * cols])


def attn_grad(xt_ref, xt2_ref, gft_ref, keep_ref, g_ref, h_ref):
    cols = keep_ref.shape[1] // 4
    g_ref[...] = mm(xt_ref[...], keep_ref[:, : 2 * cols]).astype(BF16)
    h_ref[:, :cols] = mm(xt2_ref[...], keep_ref[:, 2 * cols : 3 * cols]).astype(BF16)
    h_ref[:, cols:] = mm(gft_ref[...], keep_ref[:, 3 * cols :]).astype(BF16)


def back_body(gf_ref, xt_ref, xt2_ref, gft_ref, w_ref, saved_ref, probs_ref, ga_ref, gb_ref, keep_ref):
    term = attend_back_shard(gf_ref[...], w_ref, saved_ref, probs_ref, keep_ref)

    @pl.when(pl.program_id(0) == pl.num_programs(0) - 1)
    def _():
        attn_grad(xt_ref, xt2_ref, gft_ref, keep_ref, ga_ref, gb_ref)

    return term


def back_far_kernel(
    low_ref, gf_ref, xt_ref, xt2_ref, gft_ref, saved_ref, probs_ref, h_ref, i_ref,
    acc_ref, ga_ref, gb_ref, keep_ref, w_ref,
):
    join_pair(low_ref, ((h_ref, i_ref),), (w_ref,))
    term = back_body(gf_ref, xt_ref, xt2_ref, gft_ref, w_ref, saved_ref, probs_ref, ga_ref, gb_ref, keep_ref)
    acc_ref[...] = jnp.zeros_like(acc_ref)
    acc_ref[...] += term


def back_pair_kernel(
    low_ref, gf_ref, xt_ref, xt2_ref, gft_ref, sa_ref, pa_ref, h_ref, i_ref, sb_ref, pb_ref, w_ref, before_ref,
    acc_ref, ga_ref, gb_ref, gc_ref, gd_ref, keep_ref, joined_ref, keep2_ref,
):
    join_pair(low_ref, ((h_ref, i_ref),), (joined_ref,))
    term = back_body(gf_ref, xt_ref, xt2_ref, gft_ref, joined_ref, sa_ref, pa_ref, ga_ref, gb_ref, keep_ref)
    term += back_body(gf_ref, xt_ref, xt2_ref, gft_ref, w_ref, sb_ref, pb_ref, gc_ref, gd_ref, keep2_ref)
    acc_ref[...] = term + before_ref[...]


def back_last_kernel(
    gf_ref, xt_ref, xt2_ref, gft_ref, saved_ref, probs_ref, w_ref, before_ref, rows_ref, gfirst_ref, vec_ref,
    ig_ref, sums_ref, ga_ref, gb_ref, keep_ref,
):
    term = back_body(gf_ref, xt_ref, xt2_ref, gft_ref, w_ref, saved_ref, probs_ref, ga_ref, gb_ref, keep_ref)
    grad_in = before_ref[...] + term
    normed, inverse = layer_stats(rows_ref[...].astype(F32))
    ig_ref[...] = gfirst_ref[...] + norm_back(grad_in * vec_ref[0:1], normed, inverse)
    one = jnp.sum(grad_in * normed, axis=0, keepdims=True)
    two = jnp.sum(grad_in, axis=0, keepdims=True)
    sums = jnp.concatenate([one, two] * 4, axis=0)

    @pl.when(pl.program_id(0) == 0)
    def _():
        sums_ref[...] = sums

    @pl.when(pl.program_id(0) > 0)
    def _():
        sums_ref[...] += sums


def back_call(kernel, ops, specs, outs, out_specs, far, grads=2):
    gfl = ops[1] if far else ops[0]
    r, d = gfl.shape
    heads = d // 4 // HEAD_DIM
    _, saved_specs = saved_outputs(r, d, heads)
    grad = jax.ShapeDtypeStruct((d, d // 2), BF16)
    scratch = [pltpu.VMEM((r, d), BF16)]
    if far:
        scratch += [pltpu.VMEM((d, d), BF16)]
    if grads == 4:
        scratch += [pltpu.VMEM((r, d), BF16)]
    return pl.pallas_call(
        kernel,
        grid=(r // PATCHES,),
        out_shape=tuple(outs) + (grad,) * grads,
        in_specs=([SMEM] if far else []) + [image_block(d)] + [full((d, r))] * 3 + saved_specs + specs,
        out_specs=out_specs + [full((d, d // 2))] * grads,
        scratch_shapes=scratch,
        compiler_params=params(BIG),
        cost_estimate=cost(3 * grads),
    )(*ops)


def run_back_far(low, gfl, xt, xt2, gft, halves, saved):
    r, d = gfl.shape
    return back_call(
        back_far_kernel,
        [low, gfl, xt, xt2, gft, *saved, *halves],
        [full((d // 2, d))] * 2,
        [jax.ShapeDtypeStruct((r, d), F32)], [image_block(d)], True,
    )


def run_back_pair(low, gfl, xt, xt2, gft, halves, saved_a, weight, saved_b, acc):
    r, d = gfl.shape
    _, saved_specs = saved_outputs(r, d, d // 4 // HEAD_DIM)
    return back_call(
        back_pair_kernel,
        [low, gfl, xt, xt2, gft, *saved_a, *halves, *saved_b, weight, acc],
        [full((d // 2, d))] * 2 + saved_specs + [full((d, d)), image_block(d)],
        [jax.ShapeDtypeStruct((r, d), F32)], [image_block(d)], True, 4,
    )


def run_back_last(gfl, xt, xt2, gft, weight, saved, acc, rows, gfirst, vectors):
    r, d = gfl.shape
    return back_call(
        back_last_kernel,
        [gfl, xt, xt2, gft, *saved, weight, acc, rows, gfirst, vectors],
        [full((d, d))] + [image_block(d)] * 3 + [full(vectors.shape)],
        [jax.ShapeDtypeStruct((r, d), F32), jax.ShapeDtypeStruct((8, d), F32)],
        [image_block(d), full((8, d))], False,
    )


def swap(value, axis, bit):
    size = lax.axis_size(axis)
    return lax.ppermute(value, axis, [(i, i ^ bit) for i in range(size)])


def all_sum(value):
    for axis in ("mp", "dp"):
        bit = 1
        while bit < lax.axis_size(axis):
            value = value + swap(value, axis, bit)
            bit *= 2
    return value


def total(terms, rows=slice(None)):
    return sum(term[rows].astype(F32) for term in terms)


def meet(own, partner):
    return own, swap(partner, "mp", 1)


def upper(terms):
    return total(terms, slice(terms[0].shape[0] // 2, None)).astype(BF16)


def fold(terms, bit, sent=None):
    half = terms[0].shape[0] // 2
    back = swap(upper(terms) if sent is None else sent, "dp", 1 << bit)
    return tuple(term[:half] for term in terms) + (back,)


def finish(near, far, order):
    near = near + (swap(total(far).astype(BF16), "mp", 2),)
    for bit in order[1:]:
        near = fold(near, bit)
    return total(near)


CORRECTION = 1.0 - MOMENT_DECAY**STEP


def lamb_step(grad, master, first, second):
    first_new = MOMENT_DECAY * first + (1.0 - MOMENT_DECAY) * grad
    second_new = MOMENT_DECAY * second + (1.0 - MOMENT_DECAY) * grad * grad
    update = (
        first_new * (1.0 / CORRECTION) / (jnp.sqrt(second_new * (1.0 / CORRECTION)) + ADAM_EPS)
        + WEIGHT_DECAY * master
    )
    return first_new, second_new, update


def whole_sum(value):
    return jnp.sum(jnp.sum(value, axis=0, keepdims=True), axis=1, keepdims=True)


def spread(parts, width):
    lane = lax.broadcasted_iota(jnp.int32, (1, width), 1)
    return sum(jnp.where(lane == index, part, 0.0) for index, part in enumerate(parts))


def dense_step_kernel(*refs):
    ins, outs = refs[:8], refs[8:]
    parts = []
    for at in range(2):
        grad, master, first, second = (ref[...] for ref in ins[4 * at : 4 * at + 4])
        first_new, second_new, update = lamb_step(grad, master, first, second)
        for ref, value in zip(outs[3 * at : 3 * at + 3], (first_new, second_new, update)):
            ref[...] = value
        parts += [whole_sum(master * master), whole_sum(update * update)]
    outs[6][...] = spread(parts, outs[6].shape[1])


def run_dense_step(in_parts, down_parts):
    shape = jax.ShapeDtypeStruct(in_parts[0].shape, F32)
    width = in_parts[0].shape[1]
    return pl.pallas_call(
        dense_step_kernel,
        out_shape=(shape,) * 6 + (jax.ShapeDtypeStruct((1, width), F32),),
        compiler_params=params(BIG),
    )(*in_parts, *down_parts)


def attn_step_kernel(
    left_ref, right_ref, qm_ref, qf_ref, qs_ref, om_ref, of_ref, os_ref, sums_a_ref, sums_b_ref, squares_ref,
    qg_ref, qf_out, qs_out, qu_ref, og_ref, of_out, os_out, ou_ref, small_ref,
):
    cols = qm_ref.shape[2]
    left, right = left_ref[...], right_ref[...]
    master_square, update_square = 0.0, 0.0
    for index, grad in enumerate((left[:, :cols], left[:, cols:], right[:, :cols])):
        master = qm_ref[index]
        first_new, second_new, update = lamb_step(grad, master, qf_ref[index], qs_ref[index])
        qg_ref[index] = grad
        qf_out[index] = first_new
        qs_out[index] = second_new
        qu_ref[index] = update
        master_square += whole_sum(master * master)
        update_square += whole_sum(update * update)
    grad = right[:, cols:].T
    master = om_ref[...]
    first_new, second_new, update = lamb_step(grad, master, of_ref[...], os_ref[...])
    og_ref[...] = grad
    of_out[...] = first_new
    os_out[...] = second_new
    ou_ref[...] = update
    dense = squares_ref[...]
    parts = [
        master_square, whole_sum(master * master), dense[:, 0:1], dense[:, 2:3],
        update_square, whole_sum(update * update), dense[:, 1:2], dense[:, 3:4],
    ]
    width = small_ref.shape[1]
    small_ref[...] = jnp.concatenate(
        [sums_a_ref[0:2], sums_b_ref[0:4], spread(parts, width), jnp.zeros((1, width), F32)], axis=0
    )


def run_attn_step(left, right, qkv, out, sums_a, sums_b, squares):
    q, o = jax.ShapeDtypeStruct(qkv[0].shape, F32), jax.ShapeDtypeStruct(out[0].shape, F32)
    return pl.pallas_call(
        attn_step_kernel,
        out_shape=(q,) * 4 + (o,) * 4 + (jax.ShapeDtypeStruct(sums_a.shape, F32),),
        compiler_params=params(BIG),
    )(left, right, *qkv, *out, sums_a, sums_b, squares)


def final_kernel(*refs):
    small_ref, vec_ref, vf_ref, vs_ref = refs[:4]
    masters, updates, new = refs[4:8], refs[8:12], refs[12:16]
    vg_out, vf_out, vs_out, v_out, norms_ref = refs[16:]
    norms = jnp.sqrt(small_ref[6:7])
    lane = lax.broadcasted_iota(jnp.int32, norms_ref.shape, 1)
    row = lax.broadcasted_iota(jnp.int32, norms_ref.shape, 0)
    table = jnp.zeros(norms_ref.shape, F32)
    for index in range(4):
        weight, update = norms[:, index : index + 1], norms[:, 4 + index : 5 + index]
        trust = weight / (update + ADAM_EPS)
        new[index][...] = masters[index][...] - LEARN_RATE * trust * updates[index][...]
        for at, value in enumerate((weight, update, trust)):
            table = jnp.where((lane == index) & (row == at), value, table)
    norms_ref[...] = table
    grad = small_ref[0:6]
    first_new = MOMENT_DECAY * vf_ref[...] + (1.0 - MOMENT_DECAY) * grad
    second_new = MOMENT_DECAY * vs_ref[...] + (1.0 - MOMENT_DECAY) * grad * grad
    vg_out[...] = grad
    vf_out[...] = first_new
    vs_out[...] = second_new
    v_out[...] = vec_ref[...] - LEARN_RATE * (first_new * (1.0 / CORRECTION)) / (
        jnp.sqrt(second_new * (1.0 / CORRECTION)) + ADAM_EPS
    )


def run_final(small, vectors, vec_first, vec_second, masters, updates):
    shape = lambda value: jax.ShapeDtypeStruct(value.shape, F32)
    flat = lambda value: value.reshape(-1, value.shape[-1])
    outs = pl.pallas_call(
        final_kernel,
        out_shape=tuple(shape(flat(m)) for m in masters)
        + (shape(vectors),) * 4
        + (jax.ShapeDtypeStruct((3, 4), F32),),
        compiler_params=params(BIG),
    )(small, vectors, vec_first, vec_second, *(flat(m) for m in masters), *(flat(u) for u in updates))
    new = [value.reshape(m.shape) for value, m in zip(outs[:4], masters)]
    return new, outs[4:]


def after(value, *others):
    return lax.optimization_barrier((value,) + others)[0]


def shards(
    rows,
    cotangent,
    group_ids,
    qkv_weight,
    out_weight,
    in_weight,
    down_weight,
    vectors,
    qkv_master,
    qkv_first,
    qkv_second,
    out_master,
    out_first,
    out_second,
    in_master,
    in_first,
    in_second,
    down_master,
    down_first,
    down_second,
    vec_first,
    vec_second,
):
    count = lax.axis_size("dp")
    width = rows.shape[1]
    half = width // 2
    nbits = count.bit_length() - 1
    me = lax.axis_index("dp").astype(jnp.int32)
    rel = jnp.arange(count, dtype=jnp.int32) ^ me
    order1 = tuple(range(nbits))
    order2 = (1, 0) + order1[2:]
    pos, pos2 = (
        sum(((rel >> bit) & 1) << (nbits - 1 - place) for place, bit in enumerate(order))
        for order in (order1, order2)
    )
    low = (me & 1).reshape(1)

    onehot = (group_ids[:, None] == jnp.arange(GROUPS, dtype=jnp.int32)[None, :]).astype(F32)
    counts = jnp.sum(onehot, axis=0)
    counts = counts + swap(counts, "mp", 2)

    attn_w = jnp.concatenate(
        [jnp.swapaxes(qkv_weight, 1, 2).reshape(-1, width), out_weight], axis=0
    )
    pieces = [
        lax.dynamic_slice_in_dim(weight, low[0] * half, half, axis)
        for weight, axis in ((attn_w, 0), (in_weight, 0), (down_weight, 1))
    ]
    counts, *pieces = lax.optimization_barrier((counts, *pieces))
    attn_far, in_far, down_far = (swap(piece, "mp", 2) for piece in pieces)
    attn_one, in_one, down_one = (swap(weight, "mp", 1) for weight in (attn_w, in_weight, down_weight))
    counts = counts + swap(counts, "dp", 1)
    attn_two = (attn_far, swap(after(attn_far, counts), "dp", 1))
    in_two = (in_far, swap(in_far, "dp", 1))
    down_two = (down_far, swap(down_far, "dp", 1))
    attn_three, in_three, down_three = (
        tuple(swap(piece, "mp", 1) for piece in pieces) for pieces in (attn_two, in_two, down_two)
    )
    counts = counts + swap(counts, "mp", 1)
    for bit in order1[1:]:
        counts = counts + swap(counts, "dp", 1 << bit)
    image_weight = jnp.sqrt(jnp.sum(counts) / (GROUPS * jnp.sum(onehot * counts, axis=1)))

    x, xt, xt2 = run_start(pos, pos2, rows, vectors, count)
    xt, xt2 = turned_order(xt, pos, count), turned_order(xt2, pos2, count)
    gout, goutt = run_gout(pos2, image_weight, cotangent, count)
    goutt = turned_order(goutt, pos2, count)
    acc, s1, p1, s0, p0 = run_attn_one(after(x, in_far), rows, vectors, attn_one, attn_w)
    first, mid, midt, s3, p3, s2, p2 = run_attn_two(
        pos, low, x, acc, vectors, attn_three, attn_two, count
    )
    midt = turned_order(midt, pos, count)
    y, dm, gi1, gd1, gi0, gd0 = run_ffn_one(
        after(mid, in_two[1], down_far), midt, gout, goutt, (in_one, down_one), (in_weight, down_weight)
    )
    gi1, gd1, _ = lax.optimization_barrier((gi1, gd1, down_two[1]))
    in_near, down_near = meet(gi0, gi1), meet(gd0, gd1)
    y, in_sent, down_sent = lax.optimization_barrier((y, upper(in_near), upper(down_near)))
    in_near, down_near = fold(in_near, order1[0], in_sent), fold(down_near, order2[0], down_sent)
    out_rows, gfirst, gfl, gft, sums_b, gi3, gd3, gi2, gd2 = run_ffn_two(
        pos2, low, image_weight, mid, midt, gout, goutt,
        in_three + down_three, in_two + down_two, y, dm, first, cotangent, vectors, count,
    )
    gft = turned_order(gft, pos2, count)
    gi3, gd3, _, _ = lax.optimization_barrier((gi3, gd3, in_near[-1], down_near[-1]))
    in_far, down_far = meet(gi2, gi3), meet(gd2, gd3)
    gin, gl3, gr3 = run_back_far(low, gfl, xt, xt2, gft, attn_three, (s3, p3))
    gin, in_sent, down_sent = lax.optimization_barrier((gin, upper(in_far), upper(down_far)))
    in_far, down_far = fold(in_far, order1[0], in_sent), fold(down_far, order2[0], down_sent)
    gin, gl2, gr2, gl1, gr1 = run_back_pair(
        low, gfl, xt, xt2, gft, attn_two, (s2, p2), attn_one, (s1, p1), gin
    )
    left_far, right_far = meet(gl2, gl3), meet(gr2, gr3)
    gin, left_sent, right_sent, _, _ = lax.optimization_barrier(
        (gin, upper(left_far), upper(right_far), in_far[-1], down_far[-1])
    )
    left_far, right_far = fold(left_far, order1[0], left_sent), fold(right_far, order2[0], right_sent)
    input_grad, sums_a, gl0, gr0 = run_back_last(
        gfl, xt, xt2, gft, attn_w, (s0, p0), gin, rows, gfirst, vectors
    )
    left_near, right_near = meet(gl0, gl1), meet(gr0, gr1)
    left_near, right_near = fold(left_near, order1[0]), fold(right_near, order2[0])
    in_grad, down_grad = finish(in_near, in_far, order1), finish(down_near, down_far, order2)
    left, right = finish(left_near, left_far, order1), finish(right_near, right_far, order2)

    down_state = (down_master.T, down_first.T, down_second.T)
    in_fn, in_sn, in_up, down_fn, down_sn, down_up, squares = run_dense_step(
        (in_grad, in_master, in_first, in_second), (down_grad,) + down_state
    )
    qkv_grad, qkv_fn, qkv_sn, qkv_up, out_grad, out_fn, out_sn, out_up, small = run_attn_step(
        left, right, (qkv_master, qkv_first, qkv_second), (out_master, out_first, out_second),
        sums_a, sums_b, squares,
    )
    new, vec_outs = run_final(
        all_sum(small), vectors, vec_first, vec_second,
        (qkv_master, out_master, in_master, down_state[0]), (qkv_up, out_up, in_up, down_up),
    )
    return (
        out_rows,
        input_grad,
        qkv_grad,
        out_grad,
        in_grad,
        down_grad.T,
        qkv_fn,
        qkv_sn,
        new[0],
        out_fn,
        out_sn,
        new[1],
        in_fn,
        in_sn,
        new[2],
        down_fn.T,
        down_sn.T,
        new[3].T,
    ) + tuple(vec_outs)


def solution(mesh):
    rows = P(("dp", "mp"), None)
    qkv_state = P(None, "dp", "mp")
    out_state = P("mp", "dp")
    in_state = P("dp", "mp")
    in_specs = (
        (rows, rows, P(("dp", "mp")), P(None, None, "mp"), P("mp", None), P(None, "mp"), P("mp", None), P())
        + (qkv_state,) * 3
        + (out_state,) * 3
        + (in_state,) * 3
        + (out_state,) * 3
        + (P(), P())
    )
    out_specs = (
        (rows, rows, qkv_state, out_state, in_state, out_state)
        + (qkv_state,) * 3
        + (out_state,) * 3
        + (in_state,) * 3
        + (out_state,) * 3
        + (P(),) * 5
    )
    return jax.shard_map(shards, mesh=mesh, in_specs=in_specs, out_specs=out_specs, check_vma=False)
```

time: 342 us -> 230 us (0.67)
  waiting for transfers between devices: 154 us -> 101 us
  local copies, waits for them, and re-layouts: 48 us -> 1.51 us
  other arithmetic: 27 us -> 5.67 us
  starting transfers between devices: 36.6 us -> 48.9 us
    ppermute x37 -> x53, waiting for transfers between devices: 154 us -> 101 us  [swap(): return lax.ppermute(value, axis, [(i, i ^ bit) for i in range(size)])]
    unnamed x178 -> x48, local copies, waits for them, and re-layouts: 37.7 us -> 0.25 us
    ppermute x37 -> x53, starting transfers between devices: 36.6 us -> 48.9 us  [swap(): return lax.ppermute(value, axis, [(i, i ^ bit) for i in range(size)])]
    reduce_sum x7 -> x1, other arithmetic: 8.18 us -> 0.84 us  [shards(): counts = jnp.sum(onehot, axis=0)]
    add x11 -> x10, other arithmetic: 6.69 us -> 0.4 us  [the longest x4 0.37 us: total(): return sum((term[rows].astype(F32) for term in terms))]
    another operation x1 -> x0, local copies, waits for them, and re-layouts: 5.26 us -> none  [shards(): jnp.stack([jnp.sum(master * master) for master in masters] + [jnp.sum(ent...]
    slice x15 -> x0, local copies, waits for them, and re-layouts: 4.96 us -> none  [the longest x9 1.65 us: reduce_parts(): total[half:].astype(BF16)]
    pallas_call x2 -> x6, Pallas kernels: 23.5 us -> 28.4 us  [the longest x3 24.2 us: back_call(): pl.pallas_call(kernel, grid=(r // PATCHES,), out_shape=tuple(outs) + (gra...]
  transfers between devices with their start and end apart: 37 -> 53, of which waited for: 15 -> 30; matrix products, arithmetic and copies ran while one was open for 10% -> 3% of each run, Pallas kernels for 15% -> 29%
where the time goes in v2:
time: 230 us
  waiting for transfers between devices  101 us (44%)
  Pallas kernels  70.9 us (31%)
  starting transfers between devices  48.9 us (21%)
  other arithmetic  5.67 us (2%)
    ppermute x53, waiting for transfers between devices, swap(): return lax.ppermute(value, axis, [(i, i ^ bit) for i in range(size)])  101 us
    ppermute x53, starting transfers between devices, swap(): return lax.ppermute(value, axis, [(i, i ^ bit) for i in range(size)])  48.9 us
    pallas_call x3, Pallas kernels, back_call(): pl.pallas_call(kernel, grid=(r // PATCHES,), out_shape=tuple(outs) + (gra...  24.2 us
    pallas_call x1, Pallas kernels, run_ffn_two(): pl.pallas_call(lambda *refs: ffn_two_kernel(*refs, count=count), grid=(2...  15.1 us
    pallas_call x1, Pallas kernels, run_ffn_one(): pl.pallas_call(ffn_one_kernel, grid=(2 * TILES,), out_shape=(jax.ShapeDty...  12 us
    pallas_call x1, Pallas kernels, run_attn_two(): pl.pallas_call(lambda *refs: attn_two_kernel(*refs, count=count), grid=(r...  7.42 us
    pallas_call x1, Pallas kernels, run_attn_one(): pl.pallas_call(attn_one_kernel, grid=(r // PATCHES,), out_shape=(jax.Shap...  5.9 us
  transfers between devices with their start and end apart: 53, of which 30 were waited for; matrix products, arithmetic and copies ran while one was open for 3% of the time, Pallas kernels for 29%

profile of v2, /device:TPU:0, one launch (start us, length us, event | category | flops | bytes accessed | tf_op | source)
XLA Modules:
  0.0 229.7 jit_solution(2026961722390810954)
XLA Ops:
  1.5 3.0 %collective-permute-start = (f32[8]{0:T(128)S(1)}, f32[8]{0:T(128)S(1)}, u32[]{:S(2)}, u32[]{:S(2)}) collective-permute-start(f32[8]{0:T(128)S(1)} %convert_reduce_fusion), channel_id=1, source_target_pairs={{0,2},{1,3},{2,0},{3,1},{4,6},{5,7},{6,4},{7,5},{8,10},{9,11},{10,... | collective-permute-start | bytes 104 | tf_op jit(solution)/shard_map/ppermute | solution.py:556
  6.5 1.6 collective-permute-start.7
  8.8 1.5 collective-permute-start.1
  10.8 1.5 collective-permute-done.1
  12.3 10.5 %collective-permute-done.7.refs_7_.h_ref = bf16[384,768]{1,0:T(8,128)(2,1)S(1)} collective-permute-done((bf16[384,768]{1,0:T(8,128)(2,1)S(1)}, bf16[384,768]{1,0:T(8,128)(2,1)S(1)}, u32[]{:S(2)}, u32[]{:S(2)}) %collective-permute-start.7) | collective-permute-done | bytes 589856 | tf_op jit(solution)/shard_map/ppermute | solution.py:556
  22.8 1.5 collective-permute-start.9
  26.8 1.6 collective-permute-start.3
  28.4 2.0 collective-permute-done.3
  30.4 2.6 %collective-permute-start.4 = (f32[8]{0:T(128)S(1)}, f32[8]{0:T(128)S(1)}, u32[]{:S(2)}, u32[]{:S(2)}) collective-permute-start(f32[8]{0:T(128)S(1)} %add.245), channel_id=1, source_target_pairs={{0,16},{4,20},{8,24},{12,28},{16,0},{20,4},{24,8},{28,12},{1,17},{... | collective-permute-start | bytes 104 | tf_op jit(solution)/shard_map/ppermute | solution.py:556
  33.0 1.9 collective-permute-done.4
  37.1 1.6 collective-permute-start.14
  39.2 5.9 %shard_map.390 = (f32[512,768]{1,0:T(8,128)S(1)}, bf16[512,768]{1,0:T(8,128)(2,1)S(1)}, bf16[6,256,256]{2,1,0:T(8,128)(2,1)S(1)}, bf16[512,768]{1,0:T(8,128)(2,1)S(1)}, bf16[6,256,256]{2,1,0:T(8,128)(2,1)S(1)}) custom-call(bf16[512,768]{1,0:T(8,128)(2,1)S(1)} %get-tuple-element.115.x_ref.refs_2_, bf16[512,768]{1,0:T(8,128)(2,1)S(1)} %copy-done.6, ...), custom_call_target="tpu_custom_call" | custom-call | flops 7000000000 | bytes 21000000 | tf_op jit(solution)/shard_map/pallas_call | solution.py:237
  45.1 7.8 %collective-permute-done.14.refs_13_ = bf16[768,384]{1,0:T(8,128)(2,1)S(1)} collective-permute-done((bf16[768,384]{1,0:T(8,128)(2,1)S(1)}, bf16[768,384]{1,0:T(8,128)(2,1)S(1)}, u32[]{:S(2)}, u32[]{:S(2)}) %collective-permute-start.14) | collective-permute-done | bytes 589856 | tf_op jit(solution)/shard_map/ppermute | solution.py:556
  53.4 1.5 collective-permute-start.16
  54.9 7.4 %shard_map.391 = (f32[512,768]{1,0:T(8,128)S(1)}, bf16[512,768]{1,0:T(8,128)(2,1)S(1)}, bf16[8,96,512]{2,1,0:T(8,128)(2,1)S(1)}, bf16[512,768]{1,0:T(8,128)(2,1)...) custom-call(s32[8]{0:T(128)S(1)} %add_add_fusion.refs_0_, ...), custom_call_target="tpu_custom_call" | custom-call | flops 7000000000 | bytes 21000000 | tf_op jit(solution)/shard_map/pallas_call | solution.py:256
  62.4 6.8 %collective-permute-done.12.refs_12_ = bf16[384,768]{1,0:T(8,128)(2,1)S(1)} collective-permute-done((bf16[384,768]{1,0:T(8,128)(2,1)S(1)}, bf16[384,768]{1,0:T(8,128)(2,1)S(1)}, u32[]{:S(2)}, u32[]{:S(2)}) %collective-permute-start.12) | collective-permute-done | bytes 589856 | tf_op jit(solution)/shard_map/ppermute | solution.py:556
  69.1 12.0 %shard_map.393 = (f32[512,768]{1,0:T(8,128)S(1)}, f32[512,768]{1,0:T(8,128)S(1)}, bf16[768,768]{1,0:T(8,128)(2,1)S(1)}, bf16[768,768]{1,0:T(8,128)(2,1)S(1)}, bf...) custom-call(bf16[512,768]{1,0:T(8,128)(2,1)S(1)} %get-tuple-element.124.mid_ref.refs_3_, ...), custom_call_target="tpu_custom_call" | custom-call | flops 12999999488 | bytes 39000000 | tf_op jit(solution)/shard_map/pallas_call | solution.py:379
  82.3 1.7 collective-permute-done.20
  86.6 1.6 collective-permute-start.23
  89.1 15.1 %shard_map.394 = (bf16[512,768]{1,0:T(8,128)(2,1)}, f32[512,768]{1,0:T(8,128)S(1)}, bf16[512,768]{1,0:T(8,128)(2,1)S(1)}, bf16[8,96,512]{2,1,0:T(8,128)(2,1)S(1)...) custom-call(s32[8]{0:T(128)S(1)} %add_add_fusion.1.refs_1_.refs_0_, ...), custom_call_target="tpu_custom_call" | custom-call | flops 12999999488 | bytes 39000000 | tf_op jit(solution)/shard_map/pallas_call | solution.py:395
  104.8 5.5 %shard_map.395 = (f32[512,768]{1,0:T(8,128)S(1)}, bf16[768,384]{1,0:T(8,128)(2,1)S(1)}, bf16[768,384]{1,0:T(8,128)(2,1)S(1)}) custom-call(s32[1]{0:T(128)} %bitcast.refs_1_.low_ref, bf16[512,768]{1,0:T(8,128)(2,1)S(1)} %get-tuple-element.136.gf_ref, bf16[768,512]{1,0:T(8,128)(2,1)S(1)} %bitcast.26, bf16[768,512]{1,0:T(8,128)(2,1)S(1)} %bitcast.29, ...), custom_call_target="tpu_custom_call" | custom-call | flops 6000000000 | bytes 18000000 | tf_op jit(solution)/shard_map/pallas_call | solution.py:510
  112.0 11.1 %shard_map.396 = (f32[512,768]{1,0:T(8,128)S(1)}, bf16[768,384]{1,0:T(8,128)(2,1)S(1)}, bf16[768,384]{1,0:T(8,128)(2,1)S(1)}, bf16[768,384]{1,0:T(8,128)(2,1)S(1)}, bf16[768,384]{1,0:T(8,128)(2,1)S(1)}) custom-call(s32[1]{0:T(128)} %bitcast.refs_1_.low_ref, bf16[512,768]{1,0:T(8,128)(2,1)S(1)} %get-tuple-element.136.gf_ref, bf16[768,512]{1,0:T(8,128)(2,1)S(1)} %bitcast.27, ...), custom_call_target="tpu_custom_call" | custom-call | flops 12000000000 | bytes 36000000 | tf_op jit(solution)/shard_map/pallas_call | solution.py:510
  125.2 1.4 collective-permute-done.28
  126.9 1.6 collective-permute-start.42
  128.4 10.5 %collective-permute-done.29 = bf16[384,768]{1,0:T(8,128)(2,1)S(1)} collective-permute-done((bf16[384,768]{1,0:T(8,128)(2,1)S(1)}, bf16[384,768]{1,0:T(8,128)(2,1)S(1)}, u32[]{:S(2)}, u32[]{:S(2)}) %collective-permute-start.29) | collective-permute-done | bytes 589856 | tf_op jit(solution)/shard_map/ppermute | solution.py:556
  139.0 7.6 %shard_map.397 = (f32[512,768]{1,0:T(8,128)}, f32[8,768]{1,0:T(8,128)S(1)}, bf16[768,384]{1,0:T(8,128)(2,1)S(1)}, bf16[768,384]{1,0:T(8,128)(2,1)S(1)}) custom-call(bf16[512,768]{1,0:T(8,128)(2,1)S(1)} %get-tuple-element.136.gf_ref, bf16[768,512]{1,0:T(8,128)(2,1)S(1)} %bitcast.28, bf16[768,512]{1,0:T(8,128)(2,1)S(1)} %bitcast.31, ...), custom_call_target="tpu_custom_call" | custom-call | flops 6000000000 | bytes 18000000 | tf_op jit(solution)/shard_map/pallas_call | solution.py:510
  148.1 1.5 collective-permute-start.32
  151.2 6.9 %collective-permute-done.32 = bf16[384,384]{1,0:T(8,128)(2,1)S(1)} collective-permute-done((bf16[384,384]{1,0:T(8,128)(2,1)S(1)}, bf16[384,384]{1,0:T(8,128)(2,1)S(1)}, u32[]{:S(2)}, u32[]{:S(2)}) %collective-permute-start.32) | collective-permute-done | bytes 294944 | tf_op jit(solution)/shard_map/ppermute | solution.py:556
  158.0 1.5 collective-permute-start.45
  159.7 1.5 collective-permute-done.38
  161.2 1.5 collective-permute-start.33
  163.6 10.7 %collective-permute-done.45 = bf16[384,768]{1,0:T(8,128)(2,1)S(1)} collective-permute-done((bf16[384,768]{1,0:T(8,128)(2,1)S(1)}, bf16[384,768]{1,0:T(8,128)(2,1)S(1)}, u32[]{:S(2)}, u32[]{:S(2)}) %collective-permute-start.45) | collective-permute-done | bytes 589856 | tf_op jit(solution)/shard_map/ppermute | solution.py:556
  176.5 2.2 collective-permute-done.33
  179.5 2.3 %collective-permute-done.39 = bf16[384,384]{1,0:T(8,128)(2,1)S(1)} collective-permute-done((bf16[384,384]{1,0:T(8,128)(2,1)S(1)}, bf16[384,384]{1,0:T(8,128)(2,1)S(1)}, u32[]{:S(2)}, u32[]{:S(2)}) %collective-permute-start.39) | collective-permute-done | bytes 294944 | tf_op jit(solution)/shard_map/ppermute | solution.py:556
  181.9 1.6 collective-permute-start.40
  184.6 2.1 collective-permute-start.35
  187.2 2.7 %collective-permute-start.41 = (bf16[96,384]{1,0:T(8,128)(2,1)S(1)}, bf16[96,384]{1,0:T(8,128)(2,1)S(1)}, u32[]{:S(2)}, u32[]{:S(2)}) collective-permute-start(bf16[96,384]{1,0:T(8,128)(2,1)S(1)} %add_convert_fusion.18), channel_id=1, source_target_pairs={{0,16},{4,20},{8,24},{12,28},{16,0},{20,4},{24,8},{28,12},{1,17},{... | collective-permute-start | bytes 221192 | tf_op jit(solution)/shard_map/ppermute | solution.py:556
  190.7 5.9 %collective-permute-done.41 = bf16[96,384]{1,0:T(8,128)(2,1)S(1)} collective-permute-done((bf16[96,384]{1,0:T(8,128)(2,1)S(1)}, bf16[96,384]{1,0:T(8,128)(2,1)S(1)}, u32[]{:S(2)}, u32[]{:S(2)}) %collective-permute-start.41) | collective-permute-done | bytes 73760 | tf_op jit(solution)/shard_map/ppermute | solution.py:556
  197.0 3.0 %collective-permute-start.47 = (bf16[96,768]{1,0:T(8,128)(2,1)S(1)}, bf16[96,768]{1,0:T(8,128)(2,1)S(1)}, u32[]{:S(2)}, u32[]{:S(2)}) collective-permute-start(bf16[96,768]{1,0:T(8,128)(2,1)S(1)} %add_convert_fusion.14), channel_id=1, source_target_pairs={{0,16},{4,20},{8,24},{12,28},{16,0},{20,4},{24,8},{28,12},{1,17},{... | collective-permute-start | bytes 442376 | tf_op jit(solution)/shard_map/ppermute | solution.py:556
  200.0 4.5 %collective-permute-done.44 = bf16[96,768]{1,0:T(8,128)(2,1)S(1)} collective-permute-done((bf16[96,768]{1,0:T(8,128)(2,1)S(1)}, bf16[96,768]{1,0:T(8,128)(2,1)S(1)}, u32[]{:S(2)}, u32[]{:S(2)}) %collective-permute-start.44) | collective-permute-done | bytes 147488 | tf_op jit(solution)/shard_map/ppermute | solution.py:556
  204.6 3.0 %collective-permute-done.47 = bf16[96,768]{1,0:T(8,128)(2,1)S(1)} collective-permute-done((bf16[96,768]{1,0:T(8,128)(2,1)S(1)}, bf16[96,768]{1,0:T(8,128)(2,1)S(1)}, u32[]{:S(2)}, u32[]{:S(2)}) %collective-permute-start.47) | collective-permute-done | bytes 147488 | tf_op jit(solution)/shard_map/ppermute | solution.py:556
  207.9 1.7 shard_map.398
  209.6 1.4 shard_map.399
  212.3 1.5 collective-permute-start.49
  213.8 2.3 %collective-permute-done.49 = f32[8,768]{1,0:T(8,128)S(1)} collective-permute-done((f32[8,768]{1,0:T(8,128)S(1)}, f32[8,768]{1,0:T(8,128)S(1)}, u32[]{:S(2)}, u32[]{:S(2)}) %collective-permute-start.49) | collective-permute-done | bytes 24608 | tf_op jit(solution)/shard_map/ppermute | solution.py:556
  217.3 2.6 %collective-permute-done.50 = f32[8,768]{1,0:T(8,128)S(1)} collective-permute-done((f32[8,768]{1,0:T(8,128)S(1)}, f32[8,768]{1,0:T(8,128)S(1)}, u32[]{:S(2)}, u32[]{:S(2)}) %collective-permute-start.50) | collective-permute-done | bytes 24608 | tf_op jit(solution)/shard_map/ppermute | solution.py:556
  220.0 3.8 %collective-permute-done.51 = f32[8,768]{1,0:T(8,128)S(1)} collective-permute-done((f32[8,768]{1,0:T(8,128)S(1)}, f32[8,768]{1,0:T(8,128)S(1)}, u32[]{:S(2)}, u32[]{:S(2)}) %collective-permute-start.51) | collective-permute-done | bytes 24608 | tf_op jit(solution)/shard_map/ppermute | solution.py:556
  224.1 4.4 %collective-permute-done.52 = f32[8,768]{1,0:T(8,128)S(1)} collective-permute-done((f32[8,768]{1,0:T(8,128)S(1)}, f32[8,768]{1,0:T(8,128)S(1)}, u32[]{:S(2)}, u32[]{:S(2)}) %collective-permute-start.52) | collective-permute-done | bytes 24608 | tf_op jit(solution)/shard_map/ppermute | solution.py:556
  (161 shorter events, 32.8 us)
Async XLA Ops:
  1.5 4.9 %collective-permute-start = (f32[8]{0:T(128)S(1)}, f32[8]{0:T(128)S(1)}, u32[]{:S(2)}, u32[]{:S(2)}) collective-permute-start(f32[8]{0:T(128)S(1)} %convert_reduce_fusion), channel_id=1, source_target_pairs={{0,2},{1,3},{2,0},{3,1},{4,6},{5,7},{6,4},{7,5},{8,10},{9,11},{10,... | collective-permute-start | bytes 104 | tf_op jit(solution)/shard_map/ppermute | solution.py:556
  6.5 16.3 %collective-permute-start.7 = (bf16[384,768]{1,0:T(8,128)(2,1)S(1)}, bf16[384,768]{1,0:T(8,128)(2,1)S(1)}, u32[]{:S(2)}, u32[]{:S(2)}) collective-permute-start(bf16[384,768]{1,0:T(8,128)(2,1)S(1)} %fusion), channel_id=1, source_target_pairs={{0,2},{1,3},{2,0},{3,1},{4,6},{5,7},{6,4},{7,5},{8,10},{9,11},{10,... | collective-permute-start | bytes 1769480 | tf_op jit(solution)/shard_map/ppermute | solution.py:556
  8.2 30.5 %collective-permute-start.6 = (bf16[768,768]{1,0:T(8,128)(2,1)S(1)}, bf16[768,768]{1,0:T(8,128)(2,1)S(1)}, u32[]{:S(2)}, u32[]{:S(2)}) collective-permute-start(bf16[768,768]{1,0:T(8,128)(2,1)S(1)} %pad_maximum_fusion.wb_ref.w_ref), channel_id=1, source_target_pairs={{0,1},{1,0},{2,3},{3,2},{4,5},{5,4},{6,7},{7,6},{8,9},{9,8},{10,11... | collective-permute-start | bytes 3538952 | tf_op jit(solution)/shard_map/ppermute | solution.py:556
  8.3 60.8 %collective-permute-start.18 = (bf16[768,768]{1,0:T(8,128)(2,1)S(1)}, bf16[768,768]{1,0:T(8,128)(2,1)S(1)}, u32[]{:S(2)}, u32[]{:S(2)}) collective-permute-start(bf16[768,768]{1,0:T(8,128)(2,1)S(1)} %copy-done.12), channel_id=1, source_target_pairs={{0,1},{1,0},{2,3},{3,2},{4,5},{5,4},{6,7},{7,6},{8,9},{9,8},{10,11... | collective-permute-start | bytes 3538952 | tf_op jit(solution)/shard_map/ppermute | solution.py:556
  10.3 26.8 %collective-permute-start.5 = (bf16[384,768]{1,0:T(8,128)(2,1)S(1)}, bf16[384,768]{1,0:T(8,128)(2,1)S(1)}, u32[]{:S(2)}, u32[]{:S(2)}) collective-permute-start(bf16[384,768]{1,0:T(8,128)(2,1)S(1)} %constant_dynamic-slice_fusion.1), channel_id=1, source_target_pairs={{0,2},{1,3},{2,0},{3,1},{4,6},{5,7},{6,4},{7,5},{8,10},{9,11},{10,... | collective-permute-start | bytes 1769480 | tf_op jit(solution)/shard_map/ppermute | solution.py:556
  22.8 16.1 %collective-permute-start.9 = (bf16[384,768]{1,0:T(8,128)(2,1)S(1)}, bf16[384,768]{1,0:T(8,128)(2,1)S(1)}, u32[]{:S(2)}, u32[]{:S(2)}) collective-permute-start(bf16[384,768]{1,0:T(8,128)(2,1)S(1)} %collective-permute-done.7.refs_7_.h_ref), channel_id=1, source_target_pairs={{0,4},{4,0},{8,12},{12,8},{16,20},{20,16},{24,28},{28,24},{1,5},{5... | collective-permute-start | bytes 1769480 | tf_op jit(solution)/shard_map/ppermute | solution.py:556
  30.4 4.4 %collective-permute-start.4 = (f32[8]{0:T(128)S(1)}, f32[8]{0:T(128)S(1)}, u32[]{:S(2)}, u32[]{:S(2)}) collective-permute-start(f32[8]{0:T(128)S(1)} %add.245), channel_id=1, source_target_pairs={{0,16},{4,20},{8,24},{12,28},{16,0},{20,4},{24,8},{28,12},{1,17},{... | collective-permute-start | bytes 104 | tf_op jit(solution)/shard_map/ppermute | solution.py:556
  34.8 34.3 %collective-permute-start.19 = (bf16[768,768]{1,0:T(8,128)(2,1)S(1)}, bf16[768,768]{1,0:T(8,128)(2,1)S(1)}, u32[]{:S(2)}, u32[]{:S(2)}) collective-permute-start(bf16[768,768]{1,0:T(8,128)(2,1)S(1)} %copy-done.13), channel_id=1, source_target_pairs={{0,1},{1,0},{2,3},{3,2},{4,5},{5,4},{6,7},{7,6},{8,9},{9,8},{10,11... | collective-permute-start | bytes 3538952 | tf_op jit(solution)/shard_map/ppermute | solution.py:556
  37.1 15.8 %collective-permute-start.14 = (bf16[768,384]{1,0:T(8,128)(2,1)S(1)}, bf16[768,384]{1,0:T(8,128)(2,1)S(1)}, u32[]{:S(2)}, u32[]{:S(2)}) collective-permute-start(bf16[768,384]{1,0:T(8,128)(2,1)S(1)} %constant_dynamic-slice_fusion), channel_id=1, source_target_pairs={{0,2},{1,3},{2,0},{3,1},{4,6},{5,7},{6,4},{7,5},{8,10},{9,11},{10,... | collective-permute-start | bytes 1769480 | tf_op jit(solution)/shard_map/ppermute | solution.py:556
  38.7 14.7 %collective-permute-start.8 = (bf16[384,768]{1,0:T(8,128)(2,1)S(1)}, bf16[384,768]{1,0:T(8,128)(2,1)S(1)}, u32[]{:S(2)}, u32[]{:S(2)}) collective-permute-start(bf16[384,768]{1,0:T(8,128)(2,1)S(1)} %collective-permute-done.7.refs_7_.h_ref), channel_id=1, source_target_pairs={{0,1},{1,0},{2,3},{3,2},{4,5},{5,4},{6,7},{7,6},{8,9},{9,8},{10,11... | collective-permute-start | bytes 1769480 | tf_op jit(solution)/shard_map/ppermute | solution.py:556
  38.9 16.0 %collective-permute-start.10 = (bf16[384,768]{1,0:T(8,128)(2,1)S(1)}, bf16[384,768]{1,0:T(8,128)(2,1)S(1)}, u32[]{:S(2)}, u32[]{:S(2)}) collective-permute-start(bf16[384,768]{1,0:T(8,128)(2,1)S(1)} %collective-permute-done.9.refs_8_.i_ref), channel_id=1, source_target_pairs={{0,1},{1,0},{2,3},{3,2},{4,5},{5,4},{6,7},{7,6},{8,9},{9,8},{10,11... | collective-permute-start | bytes 1769480 | tf_op jit(solution)/shard_map/ppermute | solution.py:556
  52.9 16.2 %collective-permute-start.12 = (bf16[384,768]{1,0:T(8,128)(2,1)S(1)}, bf16[384,768]{1,0:T(8,128)(2,1)S(1)}, u32[]{:S(2)}, u32[]{:S(2)}) collective-permute-start(bf16[384,768]{1,0:T(8,128)(2,1)S(1)} %collective-permute-done.5.refs_11_), channel_id=1, source_target_pairs={{0,4},{4,0},{8,12},{12,8},{16,20},{20,16},{24,28},{28,24},{1,5},{5... | collective-permute-start | bytes 1769480 | tf_op jit(solution)/shard_map/ppermute | solution.py:556
  53.4 27.7 %collective-permute-start.16 = (bf16[768,384]{1,0:T(8,128)(2,1)S(1)}, bf16[768,384]{1,0:T(8,128)(2,1)S(1)}, u32[]{:S(2)}, u32[]{:S(2)}) collective-permute-start(bf16[768,384]{1,0:T(8,128)(2,1)S(1)} %collective-permute-done.14.refs_13_), channel_id=1, source_target_pairs={{0,4},{4,0},{8,12},{12,8},{16,20},{20,16},{24,28},{28,24},{1,5},{5... | collective-permute-start | bytes 1769480 | tf_op jit(solution)/shard_map/ppermute | solution.py:556
  81.2 4.5 %collective-permute-start.21 = (bf16[768,768]{1,0:T(8,128)(2,1)S(1)}, bf16[768,768]{1,0:T(8,128)(2,1)S(1)}, u32[]{:S(2)}, u32[]{:S(2)}) collective-permute-start(bf16[768,768]{1,0:T(8,128)(2,1)S(1)} %get-tuple-element.131), channel_id=1, source_target_pairs={{0,1},{1,0},{2,3},{3,2},{4,5},{5,4},{6,7},{7,6},{8,9},{9,8},{10,11... | collective-permute-start | bytes 3538952 | tf_op jit(solution)/shard_map/ppermute | solution.py:556
  81.7 4.9 %collective-permute-start.11 = (bf16[384,768]{1,0:T(8,128)(2,1)S(1)}, bf16[384,768]{1,0:T(8,128)(2,1)S(1)}, u32[]{:S(2)}, u32[]{:S(2)}) collective-permute-start(bf16[384,768]{1,0:T(8,128)(2,1)S(1)} %collective-permute-done.5.refs_11_), channel_id=1, source_target_pairs={{0,1},{1,0},{2,3},{3,2},{4,5},{5,4},{6,7},{7,6},{8,9},{9,8},{10,11... | collective-permute-start | bytes 1769480 | tf_op jit(solution)/shard_map/ppermute | solution.py:556
  81.8 6.4 %collective-permute-start.15 = (bf16[768,384]{1,0:T(8,128)(2,1)S(1)}, bf16[768,384]{1,0:T(8,128)(2,1)S(1)}, u32[]{:S(2)}, u32[]{:S(2)}) collective-permute-start(bf16[768,384]{1,0:T(8,128)(2,1)S(1)} %collective-permute-done.14.refs_13_), channel_id=1, source_target_pairs={{0,1},{1,0},{2,3},{3,2},{4,5},{5,4},{6,7},{7,6},{8,9},{9,8},{10,11... | collective-permute-start | bytes 1769480 | tf_op jit(solution)/shard_map/ppermute | solution.py:556
  82.2 6.0 %collective-permute-start.13 = (bf16[384,768]{1,0:T(8,128)(2,1)S(1)}, bf16[384,768]{1,0:T(8,128)(2,1)S(1)}, u32[]{:S(2)}, u32[]{:S(2)}) collective-permute-start(bf16[384,768]{1,0:T(8,128)(2,1)S(1)} %collective-permute-done.12.refs_12_), channel_id=1, source_target_pairs={{0,1},{1,0},{2,3},{3,2},{4,5},{5,4},{6,7},{7,6},{8,9},{9,8},{10,11... | collective-permute-start | bytes 1769480 | tf_op jit(solution)/shard_map/ppermute | solution.py:556
  84.1 5.1 %collective-permute-start.17 = (bf16[768,384]{1,0:T(8,128)(2,1)S(1)}, bf16[768,384]{1,0:T(8,128)(2,1)S(1)}, u32[]{:S(2)}, u32[]{:S(2)}) collective-permute-start(bf16[768,384]{1,0:T(8,128)(2,1)S(1)} %collective-permute-done.16.refs_14_), channel_id=1, source_target_pairs={{0,1},{1,0},{2,3},{3,2},{4,5},{5,4},{6,7},{7,6},{8,9},{9,8},{10,11... | collective-permute-start | bytes 1769480 | tf_op jit(solution)/shard_map/ppermute | solution.py:556
  85.9 18.4 %collective-permute-start.22 = (bf16[384,768]{1,0:T(8,128)(2,1)S(1)}, bf16[384,768]{1,0:T(8,128)(2,1)S(1)}, u32[]{:S(2)}, u32[]{:S(2)}) collective-permute-start(bf16[384,768]{1,0:T(8,128)(2,1)S(1)} %add_convert_fusion.5), channel_id=1, source_target_pairs={{0,4},{4,0},{8,12},{12,8},{16,20},{20,16},{24,28},{28,24},{1,5},{5... | collective-permute-start | bytes 1769480 | tf_op jit(solution)/shard_map/ppermute | solution.py:556
  86.6 17.7 %collective-permute-start.23 = (bf16[384,768]{1,0:T(8,128)(2,1)S(1)}, bf16[384,768]{1,0:T(8,128)(2,1)S(1)}, u32[]{:S(2)}, u32[]{:S(2)}) collective-permute-start(bf16[384,768]{1,0:T(8,128)(2,1)S(1)} %add_convert_fusion.4), channel_id=1, source_target_pairs={{0,8},{4,12},{8,0},{12,4},{16,24},{20,28},{24,16},{28,20},{1,9},{5... | collective-permute-start | bytes 1769480 | tf_op jit(solution)/shard_map/ppermute | solution.py:556
  104.3 6.6 %collective-permute-start.24 = (bf16[768,768]{1,0:T(8,128)(2,1)S(1)}, bf16[768,768]{1,0:T(8,128)(2,1)S(1)}, u32[]{:S(2)}, u32[]{:S(2)}) collective-permute-start(bf16[768,768]{1,0:T(8,128)(2,1)S(1)} %get-tuple-element.154), channel_id=1, source_target_pairs={{0,1},{1,0},{2,3},{3,2},{4,5},{5,4},{6,7},{7,6},{8,9},{9,8},{10,11... | collective-permute-start | bytes 3538952 | tf_op jit(solution)/shard_map/ppermute | solution.py:556
  104.4 6.6 %collective-permute-start.25 = (bf16[768,768]{1,0:T(8,128)(2,1)S(1)}, bf16[768,768]{1,0:T(8,128)(2,1)S(1)}, u32[]{:S(2)}, u32[]{:S(2)}) collective-permute-start(bf16[768,768]{1,0:T(8,128)(2,1)S(1)} %get-tuple-element.156), channel_id=1, source_target_pairs={{0,1},{1,0},{2,3},{3,2},{4,5},{5,4},{6,7},{7,6},{8,9},{9,8},{10,11... | collective-permute-start | bytes 3538952 | tf_op jit(solution)/shard_map/ppermute | solution.py:556
  110.3 13.4 %collective-permute-start.26 = (bf16[768,384]{1,0:T(8,128)(2,1)S(1)}, bf16[768,384]{1,0:T(8,128)(2,1)S(1)}, u32[]{:S(2)}, u32[]{:S(2)}) collective-permute-start(bf16[768,384]{1,0:T(8,128)(2,1)S(1)} %get-tuple-element.160), channel_id=1, source_target_pairs={{0,1},{1,0},{2,3},{3,2},{4,5},{5,4},{6,7},{7,6},{8,9},{9,8},{10,11... | collective-permute-start | bytes 1769480 | tf_op jit(solution)/shard_map/ppermute | solution.py:556
  110.5 14.6 %collective-permute-start.27 = (bf16[768,384]{1,0:T(8,128)(2,1)S(1)}, bf16[768,384]{1,0:T(8,128)(2,1)S(1)}, u32[]{:S(2)}, u32[]{:S(2)}) collective-permute-start(bf16[768,384]{1,0:T(8,128)(2,1)S(1)} %get-tuple-element.162), channel_id=1, source_target_pairs={{0,1},{1,0},{2,3},{3,2},{4,5},{5,4},{6,7},{7,6},{8,9},{9,8},{10,11... | collective-permute-start | bytes 1769480 | tf_op jit(solution)/shard_map/ppermute | solution.py:556
  111.2 15.4 %collective-permute-start.28 = (bf16[384,768]{1,0:T(8,128)(2,1)S(1)}, bf16[384,768]{1,0:T(8,128)(2,1)S(1)}, u32[]{:S(2)}, u32[]{:S(2)}) collective-permute-start(bf16[384,768]{1,0:T(8,128)(2,1)S(1)} %add_convert_fusion.3), channel_id=1, source_target_pairs={{0,4},{4,0},{8,12},{12,8},{16,20},{20,16},{24,28},{28,24},{1,5},{5... | collective-permute-start | bytes 1769480 | tf_op jit(solution)/shard_map/ppermute | solution.py:556
  123.1 26.5 %collective-permute-start.30 = (bf16[768,384]{1,0:T(8,128)(2,1)S(1)}, bf16[768,384]{1,0:T(8,128)(2,1)S(1)}, u32[]{:S(2)}, u32[]{:S(2)}) collective-permute-start(bf16[768,384]{1,0:T(8,128)(2,1)S(1)} %get-tuple-element.169), channel_id=1, source_target_pairs={{0,1},{1,0},{2,3},{3,2},{4,5},{5,4},{6,7},{7,6},{8,9},{9,8},{10,11... | collective-permute-start | bytes 1769480 | tf_op jit(solution)/shard_map/ppermute | solution.py:556
  123.2 23.4 %collective-permute-start.36 = (bf16[768,384]{1,0:T(8,128)(2,1)S(1)}, bf16[768,384]{1,0:T(8,128)(2,1)S(1)}, u32[]{:S(2)}, u32[]{:S(2)}) collective-permute-start(bf16[768,384]{1,0:T(8,128)(2,1)S(1)} %get-tuple-element.172), channel_id=1, source_target_pairs={{0,1},{1,0},{2,3},{3,2},{4,5},{5,4},{6,7},{7,6},{8,9},{9,8},{10,11... | collective-permute-start | bytes 1769480 | tf_op jit(solution)/shard_map/ppermute | solution.py:556
  123.7 15.3 %collective-permute-start.29 = (bf16[384,768]{1,0:T(8,128)(2,1)S(1)}, bf16[384,768]{1,0:T(8,128)(2,1)S(1)}, u32[]{:S(2)}, u32[]{:S(2)}) collective-permute-start(bf16[384,768]{1,0:T(8,128)(2,1)S(1)} %add_convert_fusion.2), channel_id=1, source_target_pairs={{0,8},{4,12},{8,0},{12,4},{16,24},{20,28},{24,16},{28,20},{1,9},{5... | collective-permute-start | bytes 1769480 | tf_op jit(solution)/shard_map/ppermute | solution.py:556
  126.9 36.0 %collective-permute-start.42 = (bf16[384,768]{1,0:T(8,128)(2,1)S(1)}, bf16[384,768]{1,0:T(8,128)(2,1)S(1)}, u32[]{:S(2)}, u32[]{:S(2)}) collective-permute-start(bf16[384,768]{1,0:T(8,128)(2,1)S(1)} %add_convert_fusion.1), channel_id=1, source_target_pairs={{0,2},{1,3},{2,0},{3,1},{4,6},{5,7},{6,4},{7,5},{8,10},{9,11},{10,... | collective-permute-start | bytes 1769480 | tf_op jit(solution)/shard_map/ppermute | solution.py:556
  146.7 32.8 %collective-permute-start.37 = (bf16[384,384]{1,0:T(8,128)(2,1)S(1)}, bf16[384,384]{1,0:T(8,128)(2,1)S(1)}, u32[]{:S(2)}, u32[]{:S(2)}) collective-permute-start(bf16[384,384]{1,0:T(8,128)(2,1)S(1)} %add_convert_fusion.9), channel_id=1, source_target_pairs={{0,8},{4,12},{8,0},{12,4},{16,24},{20,28},{24,16},{28,20},{1,9},{5... | collective-permute-start | bytes 884744 | tf_op jit(solution)/shard_map/ppermute | solution.py:556
  148.1 9.9 %collective-permute-start.32 = (bf16[384,384]{1,0:T(8,128)(2,1)S(1)}, bf16[384,384]{1,0:T(8,128)(2,1)S(1)}, u32[]{:S(2)}, u32[]{:S(2)}) collective-permute-start(bf16[384,384]{1,0:T(8,128)(2,1)S(1)} %add_convert_fusion.13), channel_id=1, source_target_pairs={{0,4},{4,0},{8,12},{12,8},{16,20},{20,16},{24,28},{28,24},{1,5},{5... | collective-permute-start | bytes 884744 | tf_op jit(solution)/shard_map/ppermute | solution.py:556
  149.7 25.5 %collective-permute-start.31 = (bf16[384,384]{1,0:T(8,128)(2,1)S(1)}, bf16[384,384]{1,0:T(8,128)(2,1)S(1)}, u32[]{:S(2)}, u32[]{:S(2)}) collective-permute-start(bf16[384,384]{1,0:T(8,128)(2,1)S(1)} %add_convert_fusion.11), channel_id=1, source_target_pairs={{0,4},{4,0},{8,12},{12,8},{16,20},{20,16},{24,28},{28,24},{1,5},{5... | collective-permute-start | bytes 884744 | tf_op jit(solution)/shard_map/ppermute | solution.py:556
  150.3 10.9 %collective-permute-start.38 = (bf16[384,384]{1,0:T(8,128)(2,1)S(1)}, bf16[384,384]{1,0:T(8,128)(2,1)S(1)}, u32[]{:S(2)}, u32[]{:S(2)}) collective-permute-start(bf16[384,384]{1,0:T(8,128)(2,1)S(1)} %add_convert_fusion.12), channel_id=1, source_target_pairs={{0,8},{4,12},{8,0},{12,4},{16,24},{20,28},{24,16},{28,20},{1,9},{5... | collective-permute-start | bytes 884744 | tf_op jit(solution)/shard_map/ppermute | solution.py:556
  158.0 16.3 %collective-permute-start.45 = (bf16[384,768]{1,0:T(8,128)(2,1)S(1)}, bf16[384,768]{1,0:T(8,128)(2,1)S(1)}, u32[]{:S(2)}, u32[]{:S(2)}) collective-permute-start(bf16[384,768]{1,0:T(8,128)(2,1)S(1)} %add_convert_fusion), channel_id=1, source_target_pairs={{0,2},{1,3},{2,0},{3,1},{4,6},{5,7},{6,4},{7,5},{8,10},{9,11},{10,... | collective-permute-start | bytes 1769480 | tf_op jit(solution)/shard_map/ppermute | solution.py:556
  161.2 17.5 %collective-permute-start.33 = (bf16[384,384]{1,0:T(8,128)(2,1)S(1)}, bf16[384,384]{1,0:T(8,128)(2,1)S(1)}, u32[]{:S(2)}, u32[]{:S(2)}) collective-permute-start(bf16[384,384]{1,0:T(8,128)(2,1)S(1)} %add_convert_fusion.10), channel_id=1, source_target_pairs={{0,2},{1,3},{2,0},{3,1},{4,6},{5,7},{6,4},{7,5},{8,10},{9,11},{10,... | collective-permute-start | bytes 884744 | tf_op jit(solution)/shard_map/ppermute | solution.py:556
  162.8 19.0 %collective-permute-start.39 = (bf16[384,384]{1,0:T(8,128)(2,1)S(1)}, bf16[384,384]{1,0:T(8,128)(2,1)S(1)}, u32[]{:S(2)}, u32[]{:S(2)}) collective-permute-start(bf16[384,384]{1,0:T(8,128)(2,1)S(1)} %add_convert_fusion.8), channel_id=1, source_target_pairs={{0,2},{1,3},{2,0},{3,1},{4,6},{5,7},{6,4},{7,5},{8,10},{9,11},{10,... | collective-permute-start | bytes 884744 | tf_op jit(solution)/shard_map/ppermute | solution.py:556
  174.3 22.4 %collective-permute-start.43 = (bf16[192,768]{1,0:T(8,128)(2,1)S(1)}, bf16[192,768]{1,0:T(8,128)(2,1)S(1)}, u32[]{:S(2)}, u32[]{:S(2)}) collective-permute-start(bf16[192,768]{1,0:T(8,128)(2,1)S(1)} %add_convert_fusion.7), channel_id=1, source_target_pairs={{0,8},{4,12},{8,0},{12,4},{16,24},{20,28},{24,16},{28,20},{1,9},{5... | collective-permute-start | bytes 884744 | tf_op jit(solution)/shard_map/ppermute | solution.py:556
  175.1 21.7 %collective-permute-start.46 = (bf16[192,768]{1,0:T(8,128)(2,1)S(1)}, bf16[192,768]{1,0:T(8,128)(2,1)S(1)}, u32[]{:S(2)}, u32[]{:S(2)}) collective-permute-start(bf16[192,768]{1,0:T(8,128)(2,1)S(1)} %add_convert_fusion.6), channel_id=1, source_target_pairs={{0,4},{4,0},{8,12},{12,8},{16,20},{20,16},{24,28},{28,24},{1,5},{5... | collective-permute-start | bytes 884744 | tf_op jit(solution)/shard_map/ppermute | solution.py:556
  178.8 5.7 %collective-permute-start.34 = (bf16[192,384]{1,0:T(8,128)(2,1)S(1)}, bf16[192,384]{1,0:T(8,128)(2,1)S(1)}, u32[]{:S(2)}, u32[]{:S(2)}) collective-permute-start(bf16[192,384]{1,0:T(8,128)(2,1)S(1)} %add_convert_fusion.17), channel_id=1, source_target_pairs={{0,8},{4,12},{8,0},{12,4},{16,24},{20,28},{24,16},{28,20},{1,9},{5... | collective-permute-start | bytes 442376 | tf_op jit(solution)/shard_map/ppermute | solution.py:556
  181.9 5.2 %collective-permute-start.40 = (bf16[192,384]{1,0:T(8,128)(2,1)S(1)}, bf16[192,384]{1,0:T(8,128)(2,1)S(1)}, u32[]{:S(2)}, u32[]{:S(2)}) collective-permute-start(bf16[192,384]{1,0:T(8,128)(2,1)S(1)} %add_convert_fusion.16), channel_id=1, source_target_pairs={{0,4},{4,0},{8,12},{12,8},{16,20},{20,16},{24,28},{28,24},{1,5},{5... | collective-permute-start | bytes 442376 | tf_op jit(solution)/shard_map/ppermute | solution.py:556
  184.6 6.1 %collective-permute-start.35 = (bf16[96,384]{1,0:T(8,128)(2,1)S(1)}, bf16[96,384]{1,0:T(8,128)(2,1)S(1)}, u32[]{:S(2)}, u32[]{:S(2)}) collective-permute-start(bf16[96,384]{1,0:T(8,128)(2,1)S(1)} %add_convert_fusion.19), channel_id=1, source_target_pairs={{0,16},{4,20},{8,24},{12,28},{16,0},{20,4},{24,8},{28,12},{1,17},{... | collective-permute-start | bytes 221192 | tf_op jit(solution)/shard_map/ppermute | solution.py:556
  187.2 9.4 %collective-permute-start.41 = (bf16[96,384]{1,0:T(8,128)(2,1)S(1)}, bf16[96,384]{1,0:T(8,128)(2,1)S(1)}, u32[]{:S(2)}, u32[]{:S(2)}) collective-permute-start(bf16[96,384]{1,0:T(8,128)(2,1)S(1)} %add_convert_fusion.18), channel_id=1, source_target_pairs={{0,16},{4,20},{8,24},{12,28},{16,0},{20,4},{24,8},{28,12},{1,17},{... | collective-permute-start | bytes 221192 | tf_op jit(solution)/shard_map/ppermute | solution.py:556
  196.8 7.7 %collective-permute-start.44 = (bf16[96,768]{1,0:T(8,128)(2,1)S(1)}, bf16[96,768]{1,0:T(8,128)(2,1)S(1)}, u32[]{:S(2)}, u32[]{:S(2)}) collective-permute-start(bf16[96,768]{1,0:T(8,128)(2,1)S(1)} %add_convert_fusion.15), channel_id=1, source_target_pairs={{0,16},{4,20},{8,24},{12,28},{16,0},{20,4},{24,8},{28,12},{1,17},{... | collective-permute-start | bytes 442376 | tf_op jit(solution)/shard_map/ppermute | solution.py:556
  197.0 10.6 %collective-permute-start.47 = (bf16[96,768]{1,0:T(8,128)(2,1)S(1)}, bf16[96,768]{1,0:T(8,128)(2,1)S(1)}, u32[]{:S(2)}, u32[]{:S(2)}) collective-permute-start(bf16[96,768]{1,0:T(8,128)(2,1)S(1)} %add_convert_fusion.14), channel_id=1, source_target_pairs={{0,16},{4,20},{8,24},{12,28},{16,0},{20,4},{24,8},{28,12},{1,17},{... | collective-permute-start | bytes 442376 | tf_op jit(solution)/shard_map/ppermute | solution.py:556
  212.3 3.8 %collective-permute-start.49 = (f32[8,768]{1,0:T(8,128)S(1)}, f32[8,768]{1,0:T(8,128)S(1)}, u32[]{:S(2)}, u32[]{:S(2)}) collective-permute-start(f32[8,768]{1,0:T(8,128)S(1)} %add.313), channel_id=1, source_target_pairs={{0,2},{1,3},{2,0},{3,1},{4,6},{5,7},{6,4},{7,5},{8,10},{9,11},{10,... | collective-permute-start | bytes 73736 | tf_op jit(solution)/shard_map/ppermute | solution.py:556
  216.1 3.8 %collective-permute-start.50 = (f32[8,768]{1,0:T(8,128)S(1)}, f32[8,768]{1,0:T(8,128)S(1)}, u32[]{:S(2)}, u32[]{:S(2)}) collective-permute-start(f32[8,768]{1,0:T(8,128)S(1)} %add.314), channel_id=1, source_target_pairs={{0,4},{4,0},{8,12},{12,8},{16,20},{20,16},{24,28},{28,24},{1,5},{5... | collective-permute-start | bytes 73736 | tf_op jit(solution)/shard_map/ppermute | solution.py:556
  219.9 3.8 %collective-permute-start.51 = (f32[8,768]{1,0:T(8,128)S(1)}, f32[8,768]{1,0:T(8,128)S(1)}, u32[]{:S(2)}, u32[]{:S(2)}) collective-permute-start(f32[8,768]{1,0:T(8,128)S(1)} %add.315), channel_id=1, source_target_pairs={{0,8},{4,12},{8,0},{12,4},{16,24},{20,28},{24,16},{28,20},{1,9},{5... | collective-permute-start | bytes 73736 | tf_op jit(solution)/shard_map/ppermute | solution.py:556
  223.8 4.7 %collective-permute-start.52 = (f32[8,768]{1,0:T(8,128)S(1)}, f32[8,768]{1,0:T(8,128)S(1)}, u32[]{:S(2)}, u32[]{:S(2)}) collective-permute-start(f32[8,768]{1,0:T(8,128)S(1)} %add.316), channel_id=1, source_target_pairs={{0,16},{4,20},{8,24},{12,28},{16,0},{20,4},{24,8},{28,12},{1,17},{... | collective-permute-start | bytes 73736 | tf_op jit(solution)/shard_map/ppermute | solution.py:556
  (29 other events, 237.0 us)
